TPU v7x, 128 devices: a whole 4x4x4 slice. The times are simulated.
128 devices in a mesh: exp: 64 (over x, y, z), tp: 2 (over core).
Axes of the slice: x: 4, y: 4, z: 4, core: 2. Of those that a mesh axis runs over, the one named last changes fastest.
Arguments:
- tokens: bfloat16 [16384, 4096], P(('exp', 'tp')), may hold values from -6 to 6
- gate_weight: bfloat16 [64, 4096, 768], P('exp', None, 'tp'), may hold values from -0.09375 to 0.09375
- up_weight: bfloat16 [64, 4096, 768], P('exp', None, 'tp'), may hold values from -0.09375 to 0.09375
- down_weight: bfloat16 [64, 768, 4096], P('exp', 'tp'), may hold values from -0.21875 to 0.21875
- routes: int32 [16384, 8], P(('exp', 'tp')), may hold values from 0 to 63, all different within a row; in each aligned block of 128 rows (0 to 127, 128 to 255, ...) at most 18 rows name the same one
- gate_probs: float32 [16384, 8], P(('exp', 'tp')), may hold values from 0.02 to 0.5
- valid_mask: int32 [16384, 8], P(('exp', 'tp')), may hold values 0 or 1
Outputs:
- mixed: bfloat16 [16384, 4096], P(('exp', 'tp'))
- score_gate: bfloat16 [64, 4096, 768], P('exp', None, 'tp')
- score_up: bfloat16 [64, 4096, 768], P('exp', None, 'tp')
- score_down: bfloat16 [64, 768, 4096], P('exp', 'tp')
Inputs may be any that keep to these rules, and one draw needn't show every extreme that they name: Among the rows of one device, no expert is named by more than 18 entries of routes, a bound that some block reaches; a row names 8 different experts.
All inputs are finite; a program needn't handle non-finite values. No bound on the sum of `valid_mask` on one device may be relied on, other than what follows from the above.
Results may differ from a plain program's by a relative error of at most 0.0065.
Values may be sent and summed in bfloat16 or wider, within the bound.
No kernel may reach another device: no remote copies, remote signals or barrier semaphores. Data moves between devices by JAX's collectives and lax.ppermute only.
A program may use at most 192 MiB of HBM per device.

v0:
```python
import jax
import jax.numpy as jnp
from jax import lax
from jax.sharding import PartitionSpec as P


def squares_by(weights, values):
    return jnp.dot(weights, jnp.square(values.astype(jnp.float32)), precision=lax.Precision.HIGHEST)


def swiglu(tok_rows, w_gate, w_up):
    gate_proj = jnp.dot(tok_rows, w_gate, preferred_element_type=jnp.float32)
    up_proj = jnp.dot(tok_rows, w_up, preferred_element_type=jnp.float32)
    return (jax.nn.silu(gate_proj) * up_proj).astype(jnp.bfloat16)


def per_device(tokens, gate_weight, up_weight, down_weight, routes, gate_probs, valid_mask):
    tok_count, top_count = routes.shape
    model_width = tokens.shape[1]
    exp_count = lax.axis_size("exp")
    slots_cap = max(2, tok_count * top_count * 9 // (8 * exp_count))
    flat_routes = routes.reshape(-1)
    live_flat = valid_mask.reshape(-1) > 0
    combine_w = jnp.where(live_flat, gate_probs.reshape(-1), 0.0)
    onehot = (
        (flat_routes[:, None] == jnp.arange(exp_count, dtype=jnp.int32)[None, :])
        & live_flat[:, None]
    ).astype(jnp.int32)
    position = jnp.sum(jnp.cumsum(onehot, axis=0) * onehot, axis=1) - 1
    target_slot = jnp.where(live_flat, flat_routes * slots_cap + position, exp_count * slots_cap)
    source_rows = tokens[jnp.arange(tok_count * top_count) // top_count]
    send_rows = (
        jnp.zeros((exp_count * slots_cap + 1, model_width), jnp.bfloat16)
        .at[target_slot]
        .set(source_rows)[:-1]
    )
    send_w = (
        jnp.zeros((exp_count * slots_cap + 1,), jnp.bfloat16)
        .at[target_slot]
        .set(combine_w.astype(jnp.bfloat16))[:-1]
    )
    recv_rows, recv_w = (
        lax.all_to_all(
            send_rows.reshape(exp_count, slots_cap, model_width),
            "exp",
            split_axis=0,
            concat_axis=0,
            tiled=True,
        ),
        lax.all_to_all(
            send_w.reshape(exp_count, slots_cap), "exp", split_axis=0, concat_axis=0, tiled=True
        ),
    )
    recv_rows = recv_rows.reshape(-1, model_width)
    recv_w = recv_w.reshape(-1)
    w_gate = gate_weight[0]
    w_up = up_weight[0]
    w_down = down_weight[0]
    all_rows, all_w = (
        lax.all_gather(recv_rows, "tp", axis=0, tiled=True),
        lax.all_gather(recv_w, "tp", axis=0, tiled=True),
    )
    hidden = swiglu(all_rows, w_gate, w_up)
    weight_f = all_w.astype(jnp.float32)
    input_sq = squares_by(weight_f, all_rows)
    hidden_sq = squares_by(weight_f, hidden)
    down_part = jnp.dot(hidden, w_down, preferred_element_type=jnp.float32)
    expert_out = lax.psum_scatter(
        lax.optimization_barrier(down_part.astype(jnp.bfloat16))
        .astype(jnp.float32)
        .astype(jnp.bfloat16),
        "tp",
        scatter_dimension=0,
        tiled=True,
    )
    returned_rows = lax.all_to_all(
        expert_out.reshape(exp_count, slots_cap, model_width),
        "exp",
        split_axis=0,
        concat_axis=0,
        tiled=True,
    )
    picked = returned_rows.reshape(-1, model_width)[
        jnp.minimum(target_slot, exp_count * slots_cap - 1)
    ]
    weighted = (combine_w[:, None] * picked.astype(jnp.float32)).reshape(
        tok_count, top_count, model_width
    )
    mixed = jnp.sum(weighted, axis=1).astype(jnp.bfloat16)
    input_norm = jnp.sqrt(input_sq)
    score_gate = (jnp.abs(w_gate.astype(jnp.float32)) * input_norm[:, None]).astype(jnp.bfloat16)
    score_up = (jnp.abs(w_up.astype(jnp.float32)) * input_norm[:, None]).astype(jnp.bfloat16)
    score_down = (jnp.abs(w_down.astype(jnp.float32)) * jnp.sqrt(hidden_sq)[:, None]).astype(
        jnp.bfloat16
    )
    return (mixed, score_gate[None], score_up[None], score_down[None])


def solution(mesh):
    in_specs = (
        P(("exp", "tp"), None),
        P("exp", None, "tp"),
        P("exp", None, "tp"),
        P("exp", "tp", None),
        P(("exp", "tp"), None),
        P(("exp", "tp"), None),
        P(("exp", "tp"), None),
    )
    out_specs = (
        P(("exp", "tp"), None),
        P("exp", None, "tp"),
        P("exp", None, "tp"),
        P("exp", "tp", None),
    )
    return jax.shard_map(
        per_device, mesh=mesh, in_specs=in_specs, out_specs=out_specs, check_vma=False
    )
```

profile of v0, /device:TPU:50, one launch (start us, length us, event | category | flops | bytes accessed | tf_op | source)
XLA Modules:
  0.0 643.9 jit_solution(5307161020596726351)
XLA Ops:
  7.2 0.0 copy-start
  7.2 0.0 all-gather.3.cloned.1.call-start
  7.2 0.8 broadcast_select_fusion
  8.0 0.1 copy.23
  8.2 0.1 gt.32
  8.3 0.1 gt.33
  8.4 0.1 gt.31
  8.5 0.7 broadcast_multiply_fusion
  9.2 0.8 copy.25
  9.9 0.1 eq.29
  10.0 0.1 eq.25
  10.1 0.1 copy.24
  10.2 0.1 mul.67
  10.4 18.0 %reduce-window.6 = s32[64,8,128]{2,1,0:T(8,128)S(1)} reduce-window(s32[64,8,128]{2,1,0:T(8,128)S(1)} %fusion.21, s32[]{:T(128)} %constant.16.clone.1), window={size=1x1x128 pad=0_0x0_0x127_0}, to_apply=%region_0.1 | reduce-window | flops 8323072 | bytes 524292 | tf_op jit(solution)/shard_map/reduce-window
  28.4 0.1 slice.20
  28.5 0.1 copy.29
  28.7 0.1 copy.30
  28.8 0.1 broadcast_add_fusion
  28.9 0.1 fusion.18
  29.0 0.0 copy-done
  29.0 7.7 %gather_fusion = bf16[1024,4096]{1,0:T(8,128)(2,1)} fusion(bf16[128,4096]{1,0:T(8,128)(2,1)S(1)} %copy-done, s32[1024]{0:T(1024)S(1)} %broadcast_clamp_fusion.1), kind=kCustom, calls=%fused_computation | custom fusion | bytes 16781312 | tf_op jit(solution)/shard_map/gather | solution.py:31
  36.8 18.7 %scatter_custom_fusion = bf16[1153,4096]{1,0:T(8,128)(2,1)} fusion(s32[1024]{0:T(1024)S(1)} %bitcast.49, bf16[1024,4096]{1,0:T(8,128)(2,1)} %gather_fusion, bf16[]{:T(256)} %constant.34.clone.1), kind=kCustom, calls=%fused_computation.14 | custom fusion | bytes 9445888 | tf_op jit(solution)/shard_map/scatter | solution.py:35
  55.5 8.6 %slice.22 = bf16[1152,4096]{1,0:T(8,128)(2,1)} slice(bf16[1153,4096]{1,0:T(8,128)(2,1)} %scatter_custom_fusion), slice={[0:1152], [0:4096]} | slice | bytes 18874368 | tf_op jit(solution)/shard_map/slice | solution.py:33
  64.1 13.9 %reshape.210 = bf16[64,18,4096]{2,1,0:T(8,128)(2,1)} reshape(bf16[1152,4096]{1,0:T(8,128)(2,1)} %slice.22) | data formatting | bytes 18874368 | tf_op jit(solution)/shard_map/reshape | solution.py:44
  78.0 150.0 %all_to_all.20 = bf16[64,18,4096]{2,1,0:T(8,128)(2,1)} all-to-all(bf16[64,18,4096]{2,1,0:T(8,128)(2,1)} %reshape.210), channel_id=1, replica_groups=mesh['exp'=64,'tp'=2] {'exp'}, dimensions={0} | all-to-all | bytes 18874368 | tf_op jit(solution)/shard_map/all_to_all | solution.py:43
  228.1 14.1 %reshape.211 = bf16[1152,4096]{1,0:T(8,128)(2,1)} reshape(bf16[64,18,4096]{2,1,0:T(8,128)(2,1)} %all_to_all.20) | data formatting | bytes 18874368 | tf_op jit(solution)/shard_map/reshape | solution.py:54
  242.2 0.0 all-gather.3.cloned.1.call-update
  242.2 0.0 reduce-scatter.2.cloned.1.call-start
  242.3 40.2 %all-gather.3.cloned.1.call-done = bf16[2304,4096]{1,0:T(8,128)(2,1)} async-done(((bf16[1152,4096]{1,0:T(8,128)(2,1)}), bf16[2304,4096]{1,0:T(8,128)(2,1)}) %all-gather.3.cloned.1.call-update) | async-done | bytes 18874384 | tf_op jit(solution)/shard_map/all_gather | solution.py:60
  282.4 17.4 %fusion.12 = f32[2304,384]{1,0:T(8,128)} fusion(bf16[2304,4096]{1,0:T(8,128)(2,1)} %all-gather.3.cloned.1.call-done, bf16[1,4096,384]{2,1,0:T(8,128)(2,1)} %param.8), kind=kOutput, calls=%fused_computation.22 | convolution fusion | flops 7247757312 | bytes 25559040 | tf_op jit(solution)/shard_map/dot_general | solution.py:12
  299.9 0.0 copy-done.2
  299.9 14.1 %fusion.6 = bf16[2304,384]{1,0:T(8,128)(2,1)} fusion(bf16[2304,4096]{1,0:T(8,128)(2,1)S(1)} %copy-done.2, f32[2304,384]{1,0:T(8,128)} %fusion.12, bf16[1,4096,384]{2,1,0:T(8,128)(2,1)} %param.9), kind=kOutput, calls=%fused_computation.16 | convolution fusion | flops 7253065728 | bytes 27328512 | tf_op jit(solution)/shard_map/dot_general | solution.py:13
  314.0 0.0 copy-done.3
  314.0 14.1 %convolution_convert_fusion = bf16[2304,4096]{1,0:T(8,128)(2,1)} fusion(bf16[2304,384]{1,0:T(8,128)(2,1)} %fusion.6, bf16[1,384,4096]{2,1,0:T(8,128)(2,1)S(1)} %copy-done.3), kind=kOutput, calls=%fused_computation.7 | convolution fusion | flops 7257194496 | bytes 23789568 | tf_op jit(solution)/shard_map/dot_general | solution.py:67
  328.1 0.0 reduce-scatter.2.cloned.1.call-update
  328.2 0.7 copy-done.8
  328.8 0.1 copy.31
  328.9 0.1 reshape.214
  329.1 7.8 %scatter_custom_fusion.1 = bf16[1153]{0:T(1024)(128)(2,1)S(1)} fusion(s32[1024]{0:T(1024)S(1)} %bitcast.50, bf16[1024]{0:T(1024)(128)(2,1)S(1)} %select_convert_fusion, bf16[]{:T(256)} %constant.34.clone.1), kind=kCustom, calls=%fused_computation.45 | custom fusion | bytes 2308 | tf_op jit(solution)/shard_map/scatter | solution.py:40
  336.8 0.8 all_to_all.16
  337.6 10.3 %all-to-all-start.2 = ((bf16[64,1,18]{2,1,0:T(2,128)(2,1)}), bf16[64,1,18]{2,1,0:T(2,128)(2,1)S(1)}, u32[]{:S(2)}, u32[]{:S(2)}) async-start(bf16[64,1,18]{2,1,0:T(2,128)(2,1)} %all_to_all.16), calls=%async_computation.3 | async-start | bytes 65536 | tf_op jit(solution)/shard_map/all_to_all | solution.py:50
  347.9 12.8 %reduce-scatter.2.cloned.1.call-done = bf16[1152,4096]{1,0:T(8,128)(2,1)} async-done(((bf16[2304,4096]{1,0:T(8,128)(2,1)}), bf16[1152,4096]{1,0:T(8,128)(2,1)}) %reduce-scatter.2.cloned.1.call-update) | async-done | bytes 9437200 | tf_op jit(solution)/shard_map/reduce_scatter | solution.py:68
  360.8 13.9 %reshape.212 = bf16[64,18,4096]{2,1,0:T(8,128)(2,1)} reshape(bf16[1152,4096]{1,0:T(8,128)(2,1)} %reduce-scatter.2.cloned.1.call-done) | data formatting | bytes 18874368 | tf_op jit(solution)/shard_map/reshape | solution.py:77
  374.7 0.0 all-to-all-done.2
  374.7 10.5 %all-to-all-start.1 = ((bf16[64,18,4096]{2,1,0:T(8,128)(2,1)}), bf16[64,18,4096]{2,1,0:T(8,128)(2,1)}, u32[]{:S(2)}, u32[]{:S(2)}) async-start(bf16[64,18,4096]{2,1,0:T(8,128)(2,1)} %reshape.212), calls=%async_computation.2 | async-start | bytes 25165824 | tf_op jit(solution)/shard_map/all_to_all | solution.py:76
  385.2 0.1 copy.22
  385.3 0.1 reduce
  385.4 0.1 reshape.249
  385.5 1.8 all-gather
  387.3 0.0 copy-start.4
  387.3 17.5 %fusion = f32[1,4096]{1,0:T(1,128)S(1)} fusion(bf16[2304,1]{0,1:T(2,128)(2,1)S(1)} %bitcast.41, bf16[2304,4096]{1,0:T(8,128)(2,1)} %all-gather.3.cloned.1.call-done), kind=kOutput, calls=%fused_computation.4 | convolution fusion | flops 132120576 | bytes 18895360 | tf_op jit(solution)/shard_map/dot_general | solution.py:8
  404.9 0.0 copy-start.6
  404.9 0.0 copy-done.7
  404.9 1.4 fusion.14
  406.4 0.0 copy-done.4
  406.4 2.6 multiply_convert_fusion
  409.0 0.0 copy-done.5
  409.0 0.0 copy-done.6
  409.0 3.5 multiply_convert_fusion.1
  412.5 176.9 %all-to-all-done.1 = bf16[64,18,4096]{2,1,0:T(8,128)(2,1)} async-done(((bf16[64,18,4096]{2,1,0:T(8,128)(2,1)}), bf16[64,18,4096]{2,1,0:T(8,128)(2,1)}, u32[]{:S(2)}, u32[]{:S(2)}) %all-to-all-start.1) | async-done | bytes 9437216 | tf_op jit(solution)/shard_map/all_to_all | solution.py:76
  589.4 14.2 %reshape.213 = bf16[1152,4096]{1,0:T(8,128)(2,1)} reshape(bf16[64,18,4096]{2,1,0:T(8,128)(2,1)} %all-to-all-done.1) | data formatting | bytes 18874368 | tf_op jit(solution)/shard_map/reshape | solution.py:83
  603.6 20.3 %gather_fusion.1 = bf16[1024,4096]{1,0:T(8,128)(2,1)} fusion(bf16[1152,4096]{1,0:T(8,128)(2,1)} %reshape.213, s32[1024]{0:T(1024)S(1)} %broadcast_clamp_fusion), kind=kCustom, calls=%fused_computation.1 | custom fusion | bytes 16781312 | tf_op jit(solution)/shard_map/gather | solution.py:83
  623.9 12.9 %fusion.3 = bf16[128,4096]{1,0:T(8,128)(2,1)} fusion(bf16[1024,4096]{1,0:T(8,128)(2,1)} %gather_fusion.1, f32[128,8]{1,0:T(8,128)S(1)} %copy.22), kind=kLoop, calls=%fused_computation.9 | loop fusion | flops 12058624 | bytes 9441280 | tf_op jit(solution)/shard_map/reduce_sum | solution.py:89
  636.8 0.0 copy-done.1
  (17 shorter events, 0.1 us)
Async XLA Ops:
  7.2 21.9 %copy-start = (bf16[128,4096]{1,0:T(8,128)(2,1)S(1)}, bf16[128,4096]{1,0:T(8,128)(2,1)}, u32[]{:S(2)}) copy-start(bf16[128,4096]{1,0:T(8,128)(2,1)} %param.7) | copy-start | bytes 3145732
  7.2 275.3 %all-gather.3.cloned.1.call-start = ((), (), s32[]{:S(2)}) async-start(), calls=%async_computation.4 | async-start | bytes 28311552 | tf_op jit(solution)/shard_map/all_gather | solution.py:60
  242.2 118.5 %reduce-scatter.2.cloned.1.call-start = ((), (), s32[]{:S(2)}) async-start(), calls=%async_computation.5 | async-start | bytes 28311552 | tf_op jit(solution)/shard_map/reduce_scatter | solution.py:68
  282.4 17.4 %copy-start.2 = (bf16[2304,4096]{1,0:T(8,128)(2,1)S(1)}, bf16[2304,4096]{1,0:T(8,128)(2,1)}, u32[]{:S(2)}) copy-start(bf16[2304,4096]{1,0:T(8,128)(2,1)} %all-gather.3.cloned.1.call-done) | copy-start | bytes 56623108
  299.9 14.1 %copy-start.3 = (bf16[1,384,4096]{2,1,0:T(8,128)(2,1)S(1)}, bf16[1,384,4096]{2,1,0:T(8,128)(2,1)}, u32[]{:S(2)}) copy-start(bf16[1,384,4096]{2,1,0:T(8,128)(2,1)} %param.10) | copy-start | bytes 9437188
  328.1 0.7 copy-start.8
  337.6 37.1 %all-to-all-start.2 = ((bf16[64,1,18]{2,1,0:T(2,128)(2,1)}), bf16[64,1,18]{2,1,0:T(2,128)(2,1)S(1)}, u32[]{:S(2)}, u32[]{:S(2)}) async-start(bf16[64,1,18]{2,1,0:T(2,128)(2,1)} %all_to_all.16), calls=%async_computation.3 | async-start | bytes 65536 | tf_op jit(solution)/shard_map/all_to_all | solution.py:50
  374.7 214.7 %all-to-all-start.1 = ((bf16[64,18,4096]{2,1,0:T(8,128)(2,1)}), bf16[64,18,4096]{2,1,0:T(8,128)(2,1)}, u32[]{:S(2)}, u32[]{:S(2)}) async-start(bf16[64,18,4096]{2,1,0:T(8,128)(2,1)} %reshape.212), calls=%async_computation.2 | async-start | bytes 25165824 | tf_op jit(solution)/shard_map/all_to_all | solution.py:76
  387.3 17.6 %copy-start.7 = (bf16[2304,384]{1,0:T(8,128)(2,1)S(1)}, bf16[2304,384]{1,0:T(8,128)(2,1)}, u32[]{:S(2)}) copy-start(bf16[2304,384]{1,0:T(8,128)(2,1)} %fusion.6) | copy-start | bytes 5308420
  387.3 19.0 %copy-start.4 = (bf16[1,384,4096]{2,1,0:T(8,128)(2,1)S(1)}, bf16[1,384,4096]{2,1,0:T(8,128)(2,1)}, u32[]{:S(2)}) copy-start(bf16[1,384,4096]{2,1,0:T(8,128)(2,1)} %param.10) | copy-start | bytes 9437188
  404.9 4.1 copy-start.5
  404.9 4.1 copy-start.6
  603.6 33.2 %copy-start.1 = (bf16[128,4096]{1,0:T(8,128)(2,1)S(1)}, bf16[128,4096]{1,0:T(8,128)(2,1)}, u32[]{:S(2)}) copy-start(bf16[128,4096]{1,0:T(8,128)(2,1)} %param.7) | copy-start | bytes 3145732
Sparse Core Ops, SparseCore 0:
  242.3 40.0 all-gather.2
  328.3 32.4 reduce-scatter.1
where the time goes:
time: 652 us; the launch traced here: 644 us
  waiting for transfers between devices  230 us (35%)
  blocking collectives  152 us (23%)
  local copies, waits for them, and re-layouts  123 us (19%)
  matrix products  64.7 us (10%)
  other arithmetic  38.9 us (6%)
  starting transfers between devices  20.9 us (3%)
  between operations  14.5 us (2%)
    all_to_all x1, waiting for transfers between devices, per_device(): lax.all_to_all(expert_out.reshape(exp_count, slots_cap, model_width), 'ex...  177 us
    all_to_all x1, blocking collectives, per_device(): lax.all_to_all(send_rows.reshape(exp_count, slots_cap, model_width), 'exp...  150 us
    all_gather x1, waiting for transfers between devices, per_device(): lax.all_gather(recv_rows, 'tp', axis=0, tiled=True)  40.2 us
    gather x1, local copies, waits for them, and re-layouts, per_device(): returned_rows.reshape(-1, model_width)  20.3 us
    dot_general x2, matrix products, squares_by(): jnp.dot(weights, jnp.square(values.astype(jnp.float32)), precision=lax.Pr...  19 us
    scatter x1, local copies, waits for them, and re-layouts, per_device(): send_rows = jnp.zeros((exp_count * slots_cap + 1, model_width), jnp.bfloa...  18.7 us
    another operation x3, other arithmetic  18.2 us
    dot_general x1, matrix products, swiglu(): gate_proj = jnp.dot(tok_rows, w_gate, preferred_element_type=jnp.float32)  17.4 us
  transfers between devices with their start and end apart: 4, of which 3 were waited for; matrix products, arithmetic and copies ran while one was open for 7% of the time, Pallas kernels for 0%

commit v1 on v0

v1 whole, which is shorter than its diff:
```python
import functools

import jax
import jax.numpy as jnp
from jax import lax
from jax.experimental import pallas as pl
from jax.experimental.pallas import tpu as pltpu
from jax.sharding import PartitionSpec as P

BF16, F32 = jnp.bfloat16, jnp.float32
CHUNK = 512
VMEM = 56 * 1024 * 1024


def iota(shape, dim):
    return lax.broadcasted_iota(jnp.int32, shape, dim)


def flip_rows(values):
    count = values.shape[0]
    eye = (iota((count, count), 0) == iota((count, count), 1)).astype(BF16)
    return lax.dot_general(values.astype(BF16), eye, (((0,), (0,)), ((), ())), preferred_element_type=F32)


def pick_chunk(chunk, base, blocks, extra, slots):
    shape = (blocks * extra, blocks * slots)
    row, col = iota(shape, 0), iota(shape, 1)
    return (col == (row // extra) * slots + chunk * extra + row % extra + base).astype(BF16)


def build_kernel(experts, slots, extra, chunks, routes, valid, probs, tok, out, slot_scr, sel_scr, acc_scr, w_scr):
    i = pl.program_id(0)
    count = routes.shape[0]
    rows = experts * slots

    def grouped(make):
        return make(slot_scr[...].reshape(experts, 1, count), iota((experts, slots, count), 1))

    @pl.when(i == 0)
    def _():
        r_t, v_t, p_t = (flip_rows(ref[...].astype(F32)) for ref in (routes, valid, probs))
        ids = iota((experts, count), 0).astype(F32)
        named, weight = jnp.zeros((experts, count), F32), jnp.zeros((experts, count), F32)
        for k in range(routes.shape[1]):
            hit = (r_t[k : k + 1, :] == ids) & (v_t[k : k + 1, :] > 0)
            named = named + jnp.where(hit, 1.0, 0.0)
            weight = weight + jnp.where(hit, p_t[k : k + 1, :], 0.0)
        before = (iota((count, count), 0) < iota((count, count), 1)).astype(BF16)
        place = jnp.dot(named.astype(BF16), before, preferred_element_type=F32)
        slot_scr[...] = jnp.where(named > 0, place, -1.0)
        hits = grouped(lambda slot, row: jnp.where(slot == row.astype(F32), 1.0, 0.0))
        sel_scr[...] = hits.reshape(rows, count).astype(BF16)
        more = grouped(
            lambda slot, row: jnp.where((slot == (row + slots).astype(F32)) & (row < extra), 1.0, 0.0)
        )
        weight = weight.reshape(experts, 1, count)
        w_main = jnp.sum(hits * weight, axis=2, keepdims=True)
        w_more = jnp.sum(more * weight, axis=2, keepdims=True)
        lane = iota((experts, slots, 128), 2)
        packed = jnp.where(lane == 0, w_main, jnp.where(lane == 1, w_more, 0.0))
        w_scr[...] = packed.reshape(rows, 128).astype(BF16)
        acc_scr[...] = jnp.zeros_like(acc_scr)

    @pl.when(i < chunks)
    def _():
        out[...] = jnp.dot(sel_scr[...], tok[...], preferred_element_type=F32).astype(BF16)
        more = grouped(
            lambda slot, row: jnp.where(
                (slot == (row % extra + slots).astype(F32)) & (row // extra == i), 1.0, 0.0
            )
        )
        acc_scr[...] += jnp.dot(
            more.reshape(rows, count).astype(BF16), tok[...], preferred_element_type=F32
        )

    @pl.when(i == chunks)
    def _():
        out[...] = acc_scr[...].astype(BF16)

    @pl.when(i == chunks + 1)
    def _():
        out[:, 0:128] = w_scr[...]


def build(routes, valid, probs, tokens, experts, slots, extra):
    count, width = tokens.shape
    chunks = width // CHUNK
    rows = experts * slots
    small = pl.BlockSpec((count, routes.shape[1]), lambda i: (0, 0))
    return pl.pallas_call(
        functools.partial(build_kernel, experts, slots, extra, chunks),
        grid=(chunks + 2,),
        in_specs=[small, small, small, pl.BlockSpec((count, CHUNK), lambda i: (0, jnp.minimum(i, chunks - 1)))],
        out_specs=pl.BlockSpec((rows, CHUNK), lambda i: (0, i)),
        out_shape=jax.ShapeDtypeStruct((rows, width + CHUNK + 128), BF16),
        scratch_shapes=[
            pltpu.VMEM((experts, count), F32),
            pltpu.VMEM((rows, count), BF16),
            pltpu.VMEM((rows, CHUNK), F32),
            pltpu.VMEM((rows, 128), BF16),
        ],
        compiler_params=pltpu.CompilerParams(vmem_limit_bytes=VMEM),
        cost_estimate=pl.CostEstimate(flops=4 * rows * count * width, bytes_accessed=2 * rows * width, transcendentals=0),
    )(routes, valid, probs, tokens)


def expert_kernel(blocks, slots, extra, chunks, x, x_more, x_w, wg0, wg1, wu0, wu1, wd0, wd1, out, sq_in, sq_hid,
                  xs, acc0, acc1, hid, w_col, acc_more):
    i = pl.program_id(0)
    rows, more = blocks * slots, blocks * extra
    half = wg0.shape[1]

    @pl.when(i == 0)
    def _():
        acc0[...] = jnp.zeros_like(acc0)
        acc1[...] = jnp.zeros_like(acc1)
        acc_more[...] = jnp.zeros_like(acc_more)
        w_main = x_w[...].astype(F32)
        w_more = jnp.dot(pick_chunk(0, 0, blocks, extra, slots), x_w[...], preferred_element_type=F32)
        w_col[0:rows, :] = jnp.broadcast_to(w_main[:, 0:1], (rows, 128))
        w_col[rows : rows + more, :] = jnp.broadcast_to(w_more[:, 1:2], (more, 128))

    @pl.when(i < chunks)
    def _():
        xs[0:rows, :] = x[...]
        xs[rows : rows + more, :] = jnp.dot(
            pick_chunk(i, 0, blocks, extra, slots), x_more[...], preferred_element_type=F32
        ).astype(BF16)
        acc0[...] += jnp.dot(xs[...], jnp.concatenate([wg0[...], wu0[...]], axis=1), preferred_element_type=F32)
        acc1[...] += jnp.dot(xs[...], jnp.concatenate([wg1[...], wu1[...]], axis=1), preferred_element_type=F32)
        for lane in range(0, CHUNK, 128):
            part = xs[:, lane : lane + 128].astype(F32)
            sq_in[:, lane : lane + 128] = jnp.sum(part * part * w_col[...], axis=0, keepdims=True)

    @pl.when(i == chunks)
    def _():
        for at, acc in ((0, acc0), (half, acc1)):
            for lane in range(0, half, 128):
                gate = acc[:, lane : lane + 128]
                up = acc[:, half + lane : half + lane + 128]
                value = (gate / (1.0 + jnp.exp(-gate)) * up).astype(BF16)
                hid[:, at + lane : at + lane + 128] = value
                value = value.astype(F32)
                sq_hid[:, at + lane : at + lane + 128] = jnp.sum(value * value * w_col[...], axis=0, keepdims=True)

    @pl.when((i >= chunks) & (i < 2 * chunks))
    def _():
        result = jnp.dot(
            hid[...], jnp.concatenate([wd0[...], wd1[...]], axis=0), preferred_element_type=F32
        ).astype(BF16)
        out[...] = result[0:rows]
        shape = (rows, more)
        row, col = iota(shape, 0), iota(shape, 1)
        spread = (row == (col // extra) * slots + (i - chunks) * extra + col % extra).astype(BF16)
        acc_more[...] += jnp.dot(spread, result[rows : rows + more], preferred_element_type=F32)

    @pl.when(i == 2 * chunks)
    def _():
        out[...] = acc_more[...].astype(BF16)


def expert(received, wg0, wg1, wu0, wu1, wd0, wd1, blocks, slots, extra):
    width, half = wg0.shape
    chunks = width // CHUNK
    rows, more = blocks * slots, blocks * extra
    up_to = lambda i: jnp.minimum(i, chunks - 1)
    after = lambda i: jnp.clip(i - chunks, 0, chunks - 1)
    w_in = pl.BlockSpec((CHUNK, half), lambda i: (up_to(i), 0))
    w_out = pl.BlockSpec((half, CHUNK), lambda i: (0, after(i)))
    return pl.pallas_call(
        functools.partial(expert_kernel, blocks, slots, extra, chunks),
        grid=(2 * chunks + 1,),
        in_specs=[
            pl.BlockSpec((rows, CHUNK), lambda i: (0, up_to(i))),
            pl.BlockSpec((rows, CHUNK), lambda i: (0, chunks)),
            pl.BlockSpec((rows, 128), lambda i: (0, (width + CHUNK) // 128)),
            w_in, w_in, w_in, w_in, w_out, w_out,
        ],
        out_specs=[
            pl.BlockSpec((rows, CHUNK), lambda i: (0, jnp.maximum(i - chunks, 0))),
            pl.BlockSpec((1, CHUNK), lambda i: (0, up_to(i))),
            pl.BlockSpec((1, 2 * half), lambda i: (0, 0)),
        ],
        out_shape=[
            jax.ShapeDtypeStruct((rows, width + CHUNK), BF16),
            jax.ShapeDtypeStruct((1, width), F32),
            jax.ShapeDtypeStruct((1, 2 * half), F32),
        ],
        scratch_shapes=[
            pltpu.VMEM((rows + more, CHUNK), BF16),
            pltpu.VMEM((rows + more, 2 * half), F32),
            pltpu.VMEM((rows + more, 2 * half), F32),
            pltpu.VMEM((rows + more, 2 * half), BF16),
            pltpu.VMEM((rows + more, 128), F32),
            pltpu.VMEM((rows, CHUNK), F32),
        ],
        compiler_params=pltpu.CompilerParams(vmem_limit_bytes=VMEM),
        cost_estimate=pl.CostEstimate(
            flops=12 * (rows + more) * width * half, bytes_accessed=4 * rows * width + 12 * width * half, transcendentals=0
        ),
    )(received, received, received, wg0, wg1, wu0, wu1, wd0, wd1)


def combine_kernel(experts, slots, extra, chunks, routes, valid, probs, x, x_more, out, slot_scr, w_scr, sel_scr):
    i = pl.program_id(0)
    count = routes.shape[0]
    rows = experts * slots
    row_of = iota((count, rows), 1) % slots

    @pl.when(i == 0)
    def _():
        ids = iota((count, experts), 1)
        named, weight = jnp.zeros((count, experts), F32), jnp.zeros((count, experts), F32)
        for k in range(routes.shape[1]):
            hit = (routes[:, k : k + 1] == ids) & (valid[:, k : k + 1] > 0)
            named = named + jnp.where(hit, 1.0, 0.0)
            weight = weight + jnp.where(hit, probs[:, k : k + 1], 0.0)
        before = (iota((count, count), 1) < iota((count, count), 0)).astype(BF16)
        place = jnp.dot(before, named.astype(BF16), preferred_element_type=F32)
        slot = jnp.where(named > 0, place, -1.0).astype(BF16)
        widen = (iota((experts, rows), 1) // slots == iota((experts, rows), 0)).astype(BF16)
        slot_scr[...] = jnp.dot(slot, widen, preferred_element_type=F32)
        w_scr[...] = jnp.dot(weight.astype(BF16), widen, preferred_element_type=F32)
        sel_scr[...] = jnp.where(slot_scr[...] == row_of.astype(F32), w_scr[...], 0.0).astype(BF16)

    more = (slot_scr[...] == (row_of % extra + slots).astype(F32)) & (row_of // extra == i)
    total = jnp.dot(sel_scr[...], x[...], preferred_element_type=F32)
    total += jnp.dot(jnp.where(more, w_scr[...], 0.0).astype(BF16), x_more[...], preferred_element_type=F32)
    out[...] = total.astype(BF16)


def combine(routes, valid, probs, returned, experts, slots, extra):
    rows, wide = returned.shape
    width = wide - CHUNK
    chunks = width // CHUNK
    count = routes.shape[0]
    small = pl.BlockSpec((count, routes.shape[1]), lambda i: (0, 0))
    return pl.pallas_call(
        functools.partial(combine_kernel, experts, slots, extra, chunks),
        grid=(chunks,),
        in_specs=[small, small, small, pl.BlockSpec((rows, CHUNK), lambda i: (0, i)),
                  pl.BlockSpec((rows, CHUNK), lambda i: (0, chunks))],
        out_specs=pl.BlockSpec((count, CHUNK), lambda i: (0, i)),
        out_shape=jax.ShapeDtypeStruct((count, width), BF16),
        scratch_shapes=[
            pltpu.VMEM((count, rows), F32),
            pltpu.VMEM((count, rows), F32),
            pltpu.VMEM((count, rows), BF16),
        ],
        compiler_params=pltpu.CompilerParams(vmem_limit_bytes=VMEM),
        cost_estimate=pl.CostEstimate(flops=4 * rows * count * width, bytes_accessed=2 * rows * wide, transcendentals=0),
    )(routes, valid, probs, returned, returned)


def swap(value):
    return lax.ppermute(value, "tp", [(0, 1), (1, 0)])


def exchange(value, experts, slots):
    value = value.reshape(experts, slots, value.shape[1])
    value = lax.all_to_all(value, "exp", split_axis=0, concat_axis=0, tiled=True)
    return value.reshape(experts * slots, value.shape[2])


def per_device(tokens, gate_weight, up_weight, down_weight, routes, gate_probs, valid_mask):
    count, top = routes.shape
    experts = lax.axis_size("exp")
    cap = max(2, count * top * 9 // (8 * experts))
    extra = 2
    slots = cap - extra
    w_gate, w_up, w_down = gate_weight[0], up_weight[0], down_weight[0]
    half = w_gate.shape[1]
    o_gate, o_up, o_down = swap(w_gate), swap(w_up), swap(w_down)
    sent = build(routes, valid_mask, gate_probs, tokens, experts, slots, extra)
    received = exchange(sent, experts, slots)
    outs, sq_in, sq_hid = expert(
        received, w_gate, o_gate, w_up, o_up, w_down, o_down, experts, slots, extra
    )
    returned = exchange(outs, experts, slots)
    mixed = combine(routes, valid_mask, gate_probs, returned, experts, slots, extra)
    other = swap(jnp.concatenate([sq_in[0], sq_hid[0, half:]]))
    both = jnp.sqrt(jnp.concatenate([sq_in[0], sq_hid[0, :half]]) + other)
    in_norm, hid_norm = both[: tokens.shape[1], None], both[tokens.shape[1] :, None]
    score_gate = (jnp.abs(w_gate.astype(F32)) * in_norm).astype(BF16)
    score_up = (jnp.abs(w_up.astype(F32)) * in_norm).astype(BF16)
    score_down = (jnp.abs(w_down.astype(F32)) * hid_norm).astype(BF16)
    return (mixed, score_gate[None], score_up[None], score_down[None])


def solution(mesh):
    in_specs = (
        P(("exp", "tp"), None),
        P("exp", None, "tp"),
        P("exp", None, "tp"),
        P("exp", "tp", None),
        P(("exp", "tp"), None),
        P(("exp", "tp"), None),
        P(("exp", "tp"), None),
    )
    out_specs = (
        P(("exp", "tp"), None),
        P("exp", None, "tp"),
        P("exp", None, "tp"),
        P("exp", "tp", None),
    )
    return jax.shard_map(
        per_device, mesh=mesh, in_specs=in_specs, out_specs=out_specs, check_vma=False
    )
```

time: 652 us -> 370 us (0.57)
  blocking collectives: 152 us -> 0 us
  local copies, waits for them, and re-layouts: 123 us -> 4.28 us
  matrix products: 64.7 us -> 0 us
  Pallas kernels: 0 us -> 57.3 us
  waiting for transfers between devices: 230 us -> 272 us
  other arithmetic: 38.9 us -> 6.07 us
  between operations: 14.5 us -> 0.77 us
    all_to_all x1 -> x0, blocking collectives: 150 us -> none  [per_device(): lax.all_to_all(send_rows.reshape(exp_count, slots_cap, model_width), 'exp...]
    all_to_all x2, waiting for transfers between devices: 177 us -> 256 us  [exchange(): lax.all_to_all(value, 'exp', split_axis=0, concat_axis=0, tiled=True)]
    dot_general x5 -> x0, matrix products: 64.7 us -> none  [the longest x2 19 us: squares_by(): jnp.dot(weights, jnp.square(values.astype(jnp.float32)), precision=lax.Pr...]
    pallas_call x0 -> x3, Pallas kernels: none -> 57.3 us  [the longest x1 37 us: expert(): pl.pallas_call(functools.partial(expert_kernel, blocks, slots, extra, chu...]
    reshape x5 -> x0, local copies, waits for them, and re-layouts: 56.3 us -> none  [the longest x1 14.2 us: per_device(): returned_rows.reshape(-1, model_width)]
    all_gather x1 -> x0, waiting for transfers between devices: 40.2 us -> none  [per_device(): lax.all_gather(recv_rows, 'tp', axis=0, tiled=True)]
    gather x2 -> x0, local copies, waits for them, and re-layouts: 28 us -> none  [the longest x1 20.3 us: per_device(): returned_rows.reshape(-1, model_width)]
    scatter x2 -> x0, local copies, waits for them, and re-layouts: 26.5 us -> none  [the longest x1 18.7 us: per_device(): send_rows = jnp.zeros((exp_count * slots_cap + 1, model_width), jnp.bfloa...]
  transfers between devices with their start and end apart: 4 -> 6, of which waited for: 3 -> 5; matrix products, arithmetic and copies ran while one was open for 7% -> 2% of each run, Pallas kernels for 0% -> 0%
where the time goes in v1:
time: 370 us; the launch traced here: 366 us
  waiting for transfers between devices  272 us (74%)
  Pallas kernels  57.3 us (15%)
  starting transfers between devices  25.8 us (7%)
  other arithmetic  6.07 us (2%)
  local copies, waits for them, and re-layouts  4.28 us (1%)
    all_to_all x2, waiting for transfers between devices, exchange(): lax.all_to_all(value, 'exp', split_axis=0, concat_axis=0, tiled=True)  256 us
    pallas_call x1, Pallas kernels, expert(): pl.pallas_call(functools.partial(expert_kernel, blocks, slots, extra, chu...  37 us
    all_to_all x2, starting transfers between devices, exchange(): lax.all_to_all(value, 'exp', split_axis=0, concat_axis=0, tiled=True)  24.8 us
    ppermute x4, waiting for transfers between devices, swap(): return lax.ppermute(value, 'tp', [(0, 1), (1, 0)])  15.6 us
    pallas_call x1, Pallas kernels, build(): pl.pallas_call(functools.partial(build_kernel, experts, slots, extra, chu...  10.6 us
    pallas_call x1, Pallas kernels, combine(): pl.pallas_call(functools.partial(combine_kernel, experts, slots, extra, c...  9.65 us
  transfers between devices with their start and end apart: 6, of which 5 were waited for; matrix products, arithmetic and copies ran while one was open for 2% of the time, Pallas kernels for 0%

profile of v1, /device:TPU:50, one launch (start us, length us, event | category | flops | bytes accessed | tf_op | source)
XLA Modules:
  0.0 366.0 jit_solution(11126633723264562538)
XLA Ops:
  0.6 1.4 copy.14.routes
  2.0 1.4 copy.15.valid
  3.4 1.4 copy.16.probs
  4.8 10.6 %shard_map.102 = bf16[1024,4736]{1,0:T(8,128)(2,1)} custom-call(s32[128,8]{1,0:T(8,128)} %copy.14.routes, s32[128,8]{1,0:T(8,128)} %copy.15.valid, f32[128,8]{1,0:T(8,128)} %copy.16.probs, bf16[128,4096]{1,0:T(8,128)(2,1)} %tok.1), custom_call_target="tpu_custom_call" | custom-call | flops 2147483648 | bytes 8388608 | tf_op jit(solution)/shard_map/pallas_call | solution.py:90
  15.5 0.0 copy-start
  15.5 11.3 %all-to-all-start = ((bf16[64,16,4736]{2,1,0:T(8,128)(2,1)}), bf16[64,16,4736]{2,1,0:T(8,128)(2,1)}, u32[]{:S(2)}, u32[]{:S(2)}) async-start(bf16[64,16,4736]{2,1,0:T(8,128)(2,1)} %bitcast.8), calls=%async_computation | async-start | bytes 19398656 | tf_op jit(solution)/shard_map/all_to_all | solution.py:261
  26.8 0.1 collective-permute-start
  26.9 0.5 collective-permute-start.1
  27.4 0.0 copy-done
  27.4 0.1 collective-permute-start.2
  27.5 5.4 %collective-permute-done.wg1 = bf16[4096,384]{1,0:T(8,128)(2,1)} collective-permute-done((bf16[4096,384]{1,0:T(8,128)(2,1)}, bf16[4096,384]{1,0:T(8,128)(2,1)}, u32[]{:S(2)}, u32[]{:S(2)}) %collective-permute-start) | collective-permute-done | bytes 3145760 | tf_op jit(solution)/shard_map/ppermute | solution.py:256
  32.9 9.0 %collective-permute-done.1.wu1 = bf16[4096,384]{1,0:T(8,128)(2,1)} collective-permute-done((bf16[4096,384]{1,0:T(8,128)(2,1)}, bf16[4096,384]{1,0:T(8,128)(2,1)}, u32[]{:S(2)}, u32[]{:S(2)}) %collective-permute-start.1) | collective-permute-done | bytes 3145760 | tf_op jit(solution)/shard_map/ppermute | solution.py:256
  41.9 0.0 collective-permute-done.2.wd1
  41.9 128.6 %all-to-all-done = bf16[64,16,4736]{2,1,0:T(8,128)(2,1)} async-done(((bf16[64,16,4736]{2,1,0:T(8,128)(2,1)}), bf16[64,16,4736]{2,1,0:T(8,128)(2,1)}, u32[]{:S(2)}, u32[]{:S(2)}) %all-to-all-start) | async-done | bytes 9699360 | tf_op jit(solution)/shard_map/all_to_all | solution.py:261
  170.5 37.0 %shard_map.103 = (bf16[1024,4608]{1,0:T(8,128)(2,1)}, f32[1,4096]{1,0:T(1,128)}, f32[1,768]{1,0:T(1,128)}) custom-call(bf16[1024,4736]{1,0:T(8,128)(2,1)} %bitcast.1.x.x_more.x_w, bf16[1024,4736]{1,0:T(8,128)(2,1)} %bitcast.1.x.x_more.x_w, bf16[1024,4736]{1,0:T(8,128)(2,1)} %bitcast.1.x.x_more.x_w, bf16[4096,384]{1,0:T(8,128)(2,1)} %bitcast.13, ...), custom_call_target="tpu_custom_call" | custom-call | flops 21743271936 | bytes 35651584 | tf_op jit(solution)/shard_map/pallas_call | solution.py:170
  207.5 0.0 copy-start.5
  207.5 0.0 copy-start.4
  207.5 0.0 copy-start.1
  207.5 13.5 %all-to-all-start.1 = ((bf16[64,16,4608]{2,1,0:T(8,128)(2,1)}), bf16[64,16,4608]{2,1,0:T(8,128)(2,1)}, u32[]{:S(2)}, u32[]{:S(2)}) async-start(bf16[64,16,4608]{2,1,0:T(8,128)(2,1)} %bitcast.9), calls=%async_computation.1 | async-start | bytes 18874368 | tf_op jit(solution)/shard_map/all_to_all | solution.py:261
  221.1 0.0 copy-start.2
  221.1 0.0 copy-start.3
  221.1 0.0 copy-done.5
  221.1 0.0 copy-done.4
  221.1 0.3 collective-permute-start.3
  221.4 1.2 collective-permute-done.3
  222.6 0.0 copy-done.1
  222.6 2.6 multiply_convert_fusion
  225.2 0.0 copy-done.2
  225.2 0.0 copy-done.3
  225.2 3.5 multiply_convert_fusion.1
  228.7 127.6 %all-to-all-done.1 = bf16[64,16,4608]{2,1,0:T(8,128)(2,1)} async-done(((bf16[64,16,4608]{2,1,0:T(8,128)(2,1)}), bf16[64,16,4608]{2,1,0:T(8,128)(2,1)}, u32[]{:S(2)}, u32[]{:S(2)}) %all-to-all-start.1) | async-done | bytes 9437216 | tf_op jit(solution)/shard_map/all_to_all | solution.py:261
  356.3 9.7 %shard_map.104 = bf16[128,4096]{1,0:T(8,128)(2,1)} custom-call(s32[128,8]{1,0:T(8,128)} %copy.14.routes, s32[128,8]{1,0:T(8,128)} %copy.15.valid, f32[128,8]{1,0:T(8,128)} %copy.16.probs, bf16[1024,4608]{1,0:T(8,128)(2,1)} %bitcast.6.x.x_more, bf16[1024,4608]{1,0:T(8,128)(2,1)} %bitcast.6.x.x_more), custom_call_target="tpu_custom_call" | custom-call | flops 2147483648 | bytes 9437184 | tf_op jit(solution)/shard_map/pallas_call | solution.py:238
  (5 shorter events, 0.0 us)
Async XLA Ops:
  15.5 11.9 %copy-start = (bf16[1,384,4096]{2,1,0:T(8,128)(2,1)S(1)}, bf16[1,384,4096]{2,1,0:T(8,128)(2,1)}, u32[]{:S(2)}) copy-start(bf16[1,384,4096]{2,1,0:T(8,128)(2,1)} %param.10) | copy-start | bytes 9437188
  15.5 155.0 %all-to-all-start = ((bf16[64,16,4736]{2,1,0:T(8,128)(2,1)}), bf16[64,16,4736]{2,1,0:T(8,128)(2,1)}, u32[]{:S(2)}, u32[]{:S(2)}) async-start(bf16[64,16,4736]{2,1,0:T(8,128)(2,1)} %bitcast.8), calls=%async_computation | async-start | bytes 19398656 | tf_op jit(solution)/shard_map/all_to_all | solution.py:261
  26.8 6.1 %collective-permute-start = (bf16[4096,384]{1,0:T(8,128)(2,1)}, bf16[4096,384]{1,0:T(8,128)(2,1)}, u32[]{:S(2)}, u32[]{:S(2)}) collective-permute-start(bf16[4096,384]{1,0:T(8,128)(2,1)} %bitcast.12), channel_id=1, source_target_pairs={{0,1},{1,0},{2,3},{3,2},{4,5},{5,4},{6,7},{7,6},{8,9},{9,8},{10,11... | collective-permute-start | bytes 9437192 | tf_op jit(solution)/shard_map/ppermute | solution.py:256
  26.9 15.0 %collective-permute-start.1 = (bf16[4096,384]{1,0:T(8,128)(2,1)}, bf16[4096,384]{1,0:T(8,128)(2,1)}, u32[]{:S(2)}, u32[]{:S(2)}) collective-permute-start(bf16[4096,384]{1,0:T(8,128)(2,1)} %bitcast.14), channel_id=1, source_target_pairs={{0,1},{1,0},{2,3},{3,2},{4,5},{5,4},{6,7},{7,6},{8,9},{9,8},{10,11... | collective-permute-start | bytes 9437192 | tf_op jit(solution)/shard_map/ppermute | solution.py:256
  27.4 14.5 %collective-permute-start.2 = (bf16[384,4096]{1,0:T(8,128)(2,1)S(1)}, bf16[384,4096]{1,0:T(8,128)(2,1)}, u32[]{:S(2)}, u32[]{:S(2)}) collective-permute-start(bf16[384,4096]{1,0:T(8,128)(2,1)S(1)} %bitcast.11), channel_id=1, source_target_pairs={{0,1},{1,0},{2,3},{3,2},{4,5},{5,4},{6,7},{7,6},{8,9},{9,8},{10,11... | collective-permute-start | bytes 9437192 | tf_op jit(solution)/shard_map/ppermute | solution.py:256
  207.5 13.6 %copy-start.5 = (f32[1,768]{1,0:T(1,128)S(1)}, f32[1,768]{1,0:T(1,128)}, u32[]{:S(2)}) copy-start(f32[1,768]{1,0:T(1,128)} %get-tuple-element.9) | copy-start | bytes 9220
  207.5 13.6 %copy-start.4 = (f32[1,4096]{1,0:T(1,128)S(1)}, f32[1,4096]{1,0:T(1,128)}, u32[]{:S(2)}) copy-start(f32[1,4096]{1,0:T(1,128)} %get-tuple-element.8) | copy-start | bytes 49156
  207.5 15.1 %copy-start.1 = (bf16[1,384,4096]{2,1,0:T(8,128)(2,1)S(1)}, bf16[1,384,4096]{2,1,0:T(8,128)(2,1)}, u32[]{:S(2)}) copy-start(bf16[1,384,4096]{2,1,0:T(8,128)(2,1)} %param.10) | copy-start | bytes 9437188
  207.5 148.8 %all-to-all-start.1 = ((bf16[64,16,4608]{2,1,0:T(8,128)(2,1)}), bf16[64,16,4608]{2,1,0:T(8,128)(2,1)}, u32[]{:S(2)}, u32[]{:S(2)}) async-start(bf16[64,16,4608]{2,1,0:T(8,128)(2,1)} %bitcast.9), calls=%async_computation.1 | async-start | bytes 18874368 | tf_op jit(solution)/shard_map/all_to_all | solution.py:261
  221.1 4.1 %copy-start.2 = (bf16[1,4096,384]{2,1,0:T(8,128)(2,1)S(1)}, bf16[1,4096,384]{2,1,0:T(8,128)(2,1)}, u32[]{:S(2)}) copy-start(bf16[1,4096,384]{2,1,0:T(8,128)(2,1)} %param.8) | copy-start | bytes 9437188
  221.1 4.1 %copy-start.3 = (bf16[1,4096,384]{2,1,0:T(8,128)(2,1)S(1)}, bf16[1,4096,384]{2,1,0:T(8,128)(2,1)}, u32[]{:S(2)}) copy-start(bf16[1,4096,384]{2,1,0:T(8,128)(2,1)} %param.9) | copy-start | bytes 9437188
  221.1 1.4 collective-permute-start.3

commit v2 on v1

v2 whole, which is shorter than its diff:
```python
import functools

import jax
import jax.numpy as jnp
from jax import lax
from jax.experimental import pallas as pl
from jax.experimental.pallas import tpu as pltpu
from jax.sharding import PartitionSpec as P

BF16, F32 = jnp.bfloat16, jnp.float32
CHUNK = 512
WIDE = 1024
VMEM = 56 * 1024 * 1024


def iota(shape, dim):
    return lax.broadcasted_iota(jnp.int32, shape, dim)


def one_hot(match):
    return jnp.where(match, 1.0, 0.0).astype(BF16)


def by_chunk(blocks, extra, slots):
    more, shape = blocks * extra, (slots // extra * blocks * extra, blocks * slots)
    row = iota((shape[0], 1), 0)
    home = (row % more) // extra * slots + row // more * extra + row % extra
    return one_hot(home == iota(shape, 1))


def by_block(blocks, extra, slots):
    more, shape = blocks * extra, (blocks * slots, slots // extra * blocks * extra)
    row = iota((shape[0], 1), 0)
    home = row % slots // extra * more + row // slots * extra + row % extra
    return one_hot(home == iota(shape, 1))


def assign(experts, routes, valid, probs):
    count = routes.shape[1]
    ids = iota((experts, count), 0)
    named, weight = jnp.zeros((experts, count), F32), jnp.zeros((experts, count), F32)
    for k in range(routes.shape[0]):
        hit = (routes[k : k + 1, :] == ids) & (valid[k : k + 1, :] > 0)
        named = named + jnp.where(hit, 1.0, 0.0)
        weight = weight + jnp.where(hit, probs[k : k + 1, :], 0.0)
    before = one_hot(iota((count, count), 0) < iota((count, count), 1))
    place = jnp.dot(named.astype(BF16), before, preferred_element_type=F32)
    return jnp.where(named > 0, place, -1.0).astype(jnp.int32), weight


def build_kernel(experts, slots, extra, chunks, routes, valid, probs, tok, out, slot_scr, sel_scr, stack, w_scr):
    i = pl.program_id(0)
    count = routes.shape[1]
    rows = experts * slots
    row = iota((experts, slots, count), 1)

    @pl.when(i == 0)
    def _():
        slot, weight = assign(experts, routes, valid, probs)
        slot_scr[...] = slot
        slot, weight = slot.reshape(experts, 1, count), weight.reshape(experts, 1, count)
        hits = slot == row
        sel_scr[...] = jnp.where(hits, 1.0, 0.0).reshape(rows, count).astype(BF16)
        w_main = jnp.sum(jnp.where(hits, weight, 0.0), axis=2, keepdims=True)
        w_more = jnp.sum(jnp.where((slot == row + slots) & (row < extra), weight, 0.0), axis=2, keepdims=True)
        lane = iota((experts, slots, 128), 2)
        packed = jnp.where(lane == 0, w_main, jnp.where(lane == 1, w_more, 0.0))
        w_scr[...] = packed.reshape(rows, 128).astype(BF16)

    @pl.when(i < chunks)
    def _():
        out[...] = jnp.dot(sel_scr[...], tok[...], preferred_element_type=F32).astype(BF16)
        for part in range(WIDE // CHUNK):
            at = pl.multiple_of((i * (WIDE // CHUNK) + part) * count, count)
            stack[pl.ds(at, count), :] = tok[:, part * CHUNK : (part + 1) * CHUNK]

    @pl.when(i == chunks)
    def _():
        slot = slot_scr[...].reshape(experts, 1, count)
        wanted = jnp.where(slot == row % extra + slots, row // extra, -1).reshape(rows, count)
        pick = jnp.concatenate([one_hot(wanted == c) for c in range(slots // extra)], axis=1)
        total = jnp.dot(pick, stack[...], preferred_element_type=F32)
        out[:, 0:CHUNK] = total.astype(BF16)
        out[:, CHUNK : CHUNK + 128] = w_scr[...]


def build(routes, valid, probs, tokens, experts, slots, extra):
    count, width = tokens.shape
    chunks = width // WIDE
    rows = experts * slots
    small = pl.BlockSpec((routes.shape[0], count), lambda i: (0, 0))
    return pl.pallas_call(
        functools.partial(build_kernel, experts, slots, extra, chunks),
        grid=(chunks + 1,),
        in_specs=[small, small, small, pl.BlockSpec((count, WIDE), lambda i: (0, jnp.minimum(i, chunks - 1)))],
        out_specs=pl.BlockSpec((rows, WIDE), lambda i: (0, i)),
        out_shape=jax.ShapeDtypeStruct((rows, width + CHUNK + 128), BF16),
        scratch_shapes=[
            pltpu.VMEM((experts, count), jnp.int32),
            pltpu.VMEM((rows, count), BF16),
            pltpu.VMEM((width // CHUNK * count, CHUNK), BF16),
            pltpu.VMEM((rows, 128), BF16),
        ],
        compiler_params=pltpu.CompilerParams(vmem_limit_bytes=VMEM),
        cost_estimate=pl.CostEstimate(flops=4 * rows * count * width, bytes_accessed=2 * rows * width, transcendentals=0),
    )(routes, valid, probs, tokens)


def unpack_kernel(blocks, slots, extra, x_more, x_w, wd, more, w_col, wd_copy):
    rows, count = blocks * slots, blocks * extra
    wd_copy[...] = wd[...]

    @pl.when(pl.program_id(0) == 0)
    def _():
        pick = by_chunk(blocks, extra, slots)
        more[...] = jnp.dot(pick, x_more[...], preferred_element_type=F32).astype(BF16)
        w_main = x_w[...].astype(F32)
        w_more = jnp.dot(pick[0:count], x_w[...], preferred_element_type=F32)
        w_col[0:rows, :] = jnp.broadcast_to(w_main[:, 0:1], (rows, 128))
        w_col[rows : rows + count, :] = jnp.broadcast_to(w_more[:, 1:2], (count, 128))


def unpack(received, wd, blocks, slots, extra):
    half, width = wd.shape
    rows, count = blocks * slots, blocks * extra
    flat = pl.BlockSpec((half, WIDE), lambda i: (0, i))
    return pl.pallas_call(
        functools.partial(unpack_kernel, blocks, slots, extra),
        grid=(width // WIDE,),
        in_specs=[
            pl.BlockSpec((rows, CHUNK), lambda i: (0, width // CHUNK)),
            pl.BlockSpec((rows, 128), lambda i: (0, (width + CHUNK) // 128)),
            flat,
        ],
        out_specs=[
            pl.BlockSpec((rows, CHUNK), lambda i: (0, 0)),
            pl.BlockSpec((rows + count, 128), lambda i: (0, 0)),
            flat,
        ],
        out_shape=[
            jax.ShapeDtypeStruct((rows, CHUNK), BF16),
            jax.ShapeDtypeStruct((rows + count, 128), F32),
            jax.ShapeDtypeStruct(wd.shape, BF16),
        ],
        compiler_params=pltpu.CompilerParams(vmem_limit_bytes=VMEM),
        cost_estimate=pl.CostEstimate(flops=2 * rows * rows * CHUNK, bytes_accessed=4 * rows * CHUNK, transcendentals=0),
    )(received, received, wd)


def hidden_kernel(blocks, slots, extra, chunks, x, x_more, w_col, wg0, wg1, wu0, wu1, hid, sq, xs, acc0, acc1):
    i = pl.program_id(0)
    rows, more = blocks * slots, blocks * extra
    half = wg0.shape[1]
    parts = WIDE // CHUNK

    @pl.when(i == 0)
    def _():
        acc0[...] = jnp.zeros_like(acc0)
        acc1[...] = jnp.zeros_like(acc1)

    @pl.when(i < chunks)
    def _():
        xs[0:rows, :] = x[...]
        for part in range(parts):
            at = pl.multiple_of((i * parts + part) * more, more)
            xs[rows : rows + more, part * CHUNK : (part + 1) * CHUNK] = x_more[pl.ds(at, more), :]
        acc0[...] += jnp.dot(xs[...], jnp.concatenate([wg0[...], wu0[...]], axis=1), preferred_element_type=F32)
        acc1[...] += jnp.dot(xs[...], jnp.concatenate([wg1[...], wu1[...]], axis=1), preferred_element_type=F32)
        for lane in range(0, WIDE, 128):
            part = xs[:, lane : lane + 128].astype(F32)
            sq[:, lane : lane + 128] = jnp.sum(part * part * w_col[...], axis=0, keepdims=True)

    @pl.when(i == chunks)
    def _():
        sq[...] = jnp.zeros_like(sq)
        for at, acc in ((0, acc0), (half, acc1)):
            for lane in range(0, half, 128):
                gate = acc[:, lane : lane + 128]
                up = acc[:, half + lane : half + lane + 128]
                value = (gate / (1.0 + jnp.exp(-gate)) * up).astype(BF16)
                hid[:, at + lane : at + lane + 128] = value
                value = value.astype(F32)
                sq[:, at + lane : at + lane + 128] = jnp.sum(value * value * w_col[...], axis=0, keepdims=True)


def hidden_units(received, x_more, w_col, wg0, wg1, wu0, wu1, blocks, slots, extra):
    width, half = wg0.shape
    chunks = width // WIDE
    rows, more = blocks * slots, blocks * extra
    up_to = lambda i: jnp.minimum(i, chunks - 1)
    w_in = pl.BlockSpec((WIDE, half), lambda i: (up_to(i), 0))
    return pl.pallas_call(
        functools.partial(hidden_kernel, blocks, slots, extra, chunks),
        grid=(chunks + 1,),
        in_specs=[
            pl.BlockSpec((rows, WIDE), lambda i: (0, up_to(i))),
            pl.BlockSpec((rows, CHUNK), lambda i: (0, 0)),
            pl.BlockSpec((rows + more, 128), lambda i: (0, 0)),
            w_in, w_in, w_in, w_in,
        ],
        out_specs=[
            pl.BlockSpec((rows + more, 2 * half), lambda i: (0, 0)),
            pl.BlockSpec((1, WIDE), lambda i: (0, i)),
        ],
        out_shape=[
            jax.ShapeDtypeStruct((rows + more, 2 * half), BF16),
            jax.ShapeDtypeStruct((1, width + WIDE), F32),
        ],
        scratch_shapes=[
            pltpu.VMEM((rows + more, WIDE), BF16),
            pltpu.VMEM((rows + more, 2 * half), F32),
            pltpu.VMEM((rows + more, 2 * half), F32),
        ],
        compiler_params=pltpu.CompilerParams(vmem_limit_bytes=VMEM),
        cost_estimate=pl.CostEstimate(
            flops=8 * (rows + more) * width * half, bytes_accessed=2 * rows * width + 8 * width * half, transcendentals=0
        ),
    )(received, x_more, w_col, wg0, wg1, wu0, wu1)


def down_kernel(blocks, slots, extra, chunks, hid, wd0, wd1, out, stack):
    i = pl.program_id(0)
    rows, more = blocks * slots, blocks * extra
    parts = WIDE // CHUNK

    @pl.when(i < chunks)
    def _():
        result = jnp.dot(
            hid[...], jnp.concatenate([wd0[...], wd1[...]], axis=0), preferred_element_type=F32
        ).astype(BF16)
        out[...] = result[0:rows]
        for part in range(parts):
            at = pl.multiple_of((i * parts + part) * more, more)
            stack[pl.ds(at, more), :] = result[rows : rows + more, part * CHUNK : (part + 1) * CHUNK]

    @pl.when(i == chunks)
    def _():
        out[:, 0:CHUNK] = jnp.dot(
            by_block(blocks, extra, slots), stack[...], preferred_element_type=F32
        ).astype(BF16)


def down(hid, wd0, wd1, blocks, slots, extra):
    half, width = wd0.shape
    chunks = width // WIDE
    rows = blocks * slots
    w_out = pl.BlockSpec((half, WIDE), lambda i: (0, jnp.minimum(i, chunks - 1)))
    return pl.pallas_call(
        functools.partial(down_kernel, blocks, slots, extra, chunks),
        grid=(chunks + 1,),
        in_specs=[pl.BlockSpec(hid.shape, lambda i: (0, 0)), w_out, w_out],
        out_specs=pl.BlockSpec((rows, WIDE), lambda i: (0, i)),
        out_shape=jax.ShapeDtypeStruct((rows, width + CHUNK), BF16),
        scratch_shapes=[pltpu.VMEM((rows, CHUNK), BF16)],
        compiler_params=pltpu.CompilerParams(vmem_limit_bytes=VMEM),
        cost_estimate=pl.CostEstimate(
            flops=4 * hid.shape[0] * width * half, bytes_accessed=2 * rows * width + 4 * width * half, transcendentals=0
        ),
    )(hid, wd0, wd1)


def after(value, *first):
    anywhere = pl.BlockSpec(memory_space=pl.ANY)
    return pl.pallas_call(
        lambda *refs: None,
        in_specs=[anywhere] * (1 + len(first)),
        out_specs=anywhere,
        out_shape=jax.ShapeDtypeStruct(value.shape, value.dtype),
        input_output_aliases={0: 0},
        cost_estimate=pl.CostEstimate(flops=0, bytes_accessed=0, transcendentals=0),
    )(value, *first)


def column(line):
    eye = iota((128, 128), 0) == iota((128, 128), 1)
    return jnp.concatenate(
        [
            jnp.sum(jnp.where(eye, line[:, at : at + 128], 0.0), axis=1, keepdims=True)
            for at in range(0, line.shape[1], 128)
        ],
        axis=0,
    )


def combine_kernel(experts, slots, extra, chunks, routes, valid, probs, x, x_more, own, other, own_hid, other_hid, wg, wu, wd,
                   out, s_gate, s_up, s_down, sel_scr, more_scr, stack):
    i = pl.program_id(0)
    count = routes.shape[1]
    rows, more = experts * slots, experts * extra

    @pl.when(i == 0)
    def _():
        slot, weight = assign(experts, routes, valid, probs)
        slot, weight = slot.reshape(experts, 1, count), weight.reshape(experts, 1, count)
        hits = slot == iota((experts, slots, count), 1)
        sel_scr[...] = jnp.where(hits, weight, 0.0).reshape(rows, count).T.astype(BF16)
        late = [jnp.where(slot == slots + r, weight, 0.0).reshape(experts, count) for r in range(extra)]
        widen = [one_hot(iota((more, experts), 0) == iota((more, experts), 1) * extra + r) for r in range(extra)]
        spread = sum(
            jnp.dot(w, l.astype(BF16), preferred_element_type=F32) for w, l in zip(widen, late)
        )
        more_scr[...] = spread.T.astype(BF16)
        stack[...] = jnp.dot(
            by_chunk(experts, extra, slots), x_more[...], preferred_element_type=F32
        ).astype(BF16)

    total = jnp.dot(sel_scr[...], x[...], preferred_element_type=F32)
    for part in range(WIDE // CHUNK):
        at = pl.multiple_of((i * (WIDE // CHUNK) + part) * more, more)
        lanes = slice(part * CHUNK, (part + 1) * CHUNK)
        out[:, lanes] = (
            total[:, lanes]
            + jnp.dot(more_scr[...], stack[pl.ds(at, more), :], preferred_element_type=F32)
        ).astype(BF16)
    norm = column(jnp.sqrt(own[...] + other[...]))
    s_gate[...] = (jnp.abs(wg[...].astype(F32)) * norm).astype(BF16)
    s_up[...] = (jnp.abs(wu[...].astype(F32)) * norm).astype(BF16)
    half = wg.shape[1]
    norm = column(jnp.sqrt(own_hid[:, 0:half] + other_hid[:, half : 2 * half]))
    s_down[...] = (jnp.abs(wd[...].astype(F32)) * norm).astype(BF16)


def combine(routes, valid, probs, returned, own, other, wg, wu, wd, experts, slots, extra):
    rows, wide = returned.shape
    width = wide - CHUNK
    chunks = width // WIDE
    count, half = routes.shape[1], wg.shape[1]
    small = pl.BlockSpec((routes.shape[0], count), lambda i: (0, 0))
    tall = pl.BlockSpec((WIDE, half), lambda i: (i, 0))
    flat = pl.BlockSpec((half, WIDE), lambda i: (0, i))
    sums = pl.BlockSpec((1, WIDE), lambda i: (0, i))
    last = pl.BlockSpec((1, WIDE), lambda i: (0, chunks))
    return pl.pallas_call(
        functools.partial(combine_kernel, experts, slots, extra, chunks),
        grid=(chunks,),
        in_specs=[
            small, small, small,
            pl.BlockSpec((rows, WIDE), lambda i: (0, i)),
            pl.BlockSpec((rows, CHUNK), lambda i: (0, width // CHUNK)),
            sums, sums, last, last,
            tall, tall, flat,
        ],
        out_specs=[pl.BlockSpec((count, WIDE), lambda i: (0, i)), tall, tall, flat],
        out_shape=[
            jax.ShapeDtypeStruct((count, width), BF16),
            jax.ShapeDtypeStruct(wg.shape, BF16),
            jax.ShapeDtypeStruct(wu.shape, BF16),
            jax.ShapeDtypeStruct(wd.shape, BF16),
        ],
        scratch_shapes=[
            pltpu.VMEM((count, rows), BF16),
            pltpu.VMEM((count, experts * extra), BF16),
            pltpu.VMEM((rows, CHUNK), BF16),
        ],
        compiler_params=pltpu.CompilerParams(vmem_limit_bytes=VMEM),
        cost_estimate=pl.CostEstimate(flops=4 * rows * count * width, bytes_accessed=6 * rows * wide, transcendentals=0),
    )(routes, valid, probs, returned, returned, own, other, own, other, wg, wu, wd)


def swap(value):
    return lax.ppermute(value, "tp", [(0, 1), (1, 0)])


def exchange(value, experts, slots):
    value = value.reshape(experts, slots, value.shape[1])
    value = lax.all_to_all(value, "exp", split_axis=0, concat_axis=0, tiled=True)
    return value.reshape(experts * slots, value.shape[2])


def per_device(tokens, gate_weight, up_weight, down_weight, routes, gate_probs, valid_mask):
    count, top = routes.shape
    experts = lax.axis_size("exp")
    cap = max(2, count * top * 9 // (8 * experts))
    extra = 2
    slots = cap - extra
    w_gate, w_up, w_down = gate_weight[0], up_weight[0], down_weight[0]
    o_gate, o_up = swap(w_gate), swap(w_up)
    routes, valid_mask, gate_probs = routes.T, valid_mask.T, gate_probs.T
    sent = build(routes, valid_mask, gate_probs, tokens, experts, slots, extra)
    received = exchange(after(sent, o_gate, o_up), experts, slots)
    more, w_col, late_down = unpack(received, w_down, experts, slots, extra)
    o_down = swap(late_down)
    hid, sums = hidden_units(received, more, w_col, w_gate, o_gate, w_up, o_up, experts, slots, extra)
    other = swap(sums)
    outs = after(down(hid, w_down, o_down, experts, slots, extra), other)
    returned = exchange(outs, experts, slots)
    mixed, score_gate, score_up, score_down = combine(
        routes, valid_mask, gate_probs, returned, sums, other, w_gate, w_up, w_down, experts, slots, extra
    )
    return (mixed, score_gate[None], score_up[None], score_down[None])


def solution(mesh):
    in_specs = (
        P(("exp", "tp"), None),
        P("exp", None, "tp"),
        P("exp", None, "tp"),
        P("exp", "tp", None),
        P(("exp", "tp"), None),
        P(("exp", "tp"), None),
        P(("exp", "tp"), None),
    )
    out_specs = (
        P(("exp", "tp"), None),
        P("exp", None, "tp"),
        P("exp", None, "tp"),
        P("exp", "tp", None),
    )
    return jax.shard_map(
        per_device, mesh=mesh, in_specs=in_specs, out_specs=out_specs, check_vma=False
    )
```

time: 370 us -> 311 us (0.84)
  waiting for transfers between devices: 272 us -> 1.95 us
  blocking collectives: 0 us -> 236 us
  starting transfers between devices: 25.8 us -> 1.07 us
  other arithmetic: 6.07 us -> 0 us
  Pallas kernels: 57.3 us -> 62.7 us
    all_to_all x2 -> x0, waiting for transfers between devices: 256 us -> none  [exchange(): lax.all_to_all(value, 'exp', split_axis=0, concat_axis=0, tiled=True)]
    all_to_all x0 -> x2, blocking collectives: none -> 236 us  [exchange(): lax.all_to_all(value, 'exp', split_axis=0, concat_axis=0, tiled=True)]
    all_to_all x2 -> x0, starting transfers between devices: 24.8 us -> none  [exchange(): lax.all_to_all(value, 'exp', split_axis=0, concat_axis=0, tiled=True)]
    ppermute x4, waiting for transfers between devices: 15.6 us -> 1.95 us  [swap(): return lax.ppermute(value, 'tp', [(0, 1), (1, 0)])]
    convert_element_type x2 -> x0, other arithmetic: 6.06 us -> none  [the longest x1 3.5 us: per_device(): score_up = (jnp.abs(w_up.astype(F32)) * in_norm).astype(BF16)]
    pallas_call x1 -> x5, Pallas kernels: 37 us -> 42.1 us  [the longest x1 23 us: hidden_units(): pl.pallas_call(functools.partial(hidden_kernel, blocks, slots, extra, chu...]
  transfers between devices with their start and end apart: 6 -> 4, of which waited for: 5 -> 2; matrix products, arithmetic and copies ran while one was open for 2% -> 0% of each run, Pallas kernels for 0% -> 14%
where the time goes in v2:
time: 311 us; the launch traced here: 305 us
  blocking collectives  236 us (76%)
  Pallas kernels  62.7 us (20%)
    all_to_all x2, blocking collectives, exchange(): lax.all_to_all(value, 'exp', split_axis=0, concat_axis=0, tiled=True)  236 us
    pallas_call x1, Pallas kernels, hidden_units(): pl.pallas_call(functools.partial(hidden_kernel, blocks, slots, extra, chu...  23 us
    pallas_call x1, Pallas kernels, down(): pl.pallas_call(functools.partial(down_kernel, blocks, slots, extra, chunk...  12.6 us
    pallas_call x1, Pallas kernels, combine(): pl.pallas_call(functools.partial(combine_kernel, experts, slots, extra, c...  12.5 us
    pallas_call x1, Pallas kernels, build(): pl.pallas_call(functools.partial(build_kernel, experts, slots, extra, chu...  8.04 us
    pallas_call x1, Pallas kernels, unpack(): pl.pallas_call(functools.partial(unpack_kernel, blocks, slots, extra), gr...  6.5 us
  transfers between devices with their start and end apart: 4, of which 2 were waited for; matrix products, arithmetic and copies ran while one was open for 0% of the time, Pallas kernels for 14%

profile of v2, /device:TPU:50, one launch (start us, length us, event | category | flops | bytes accessed | tf_op | source)
XLA Modules:
  0.0 305.1 jit_solution(15886098788156627488)
XLA Ops:
  0.6 0.1 collective-permute-start
  0.7 0.5 collective-permute-start.1
  1.2 8.0 %shard_map.102.refs_0_ = bf16[1024,4736]{1,0:T(8,128)(2,1)} custom-call(s32[8,128]{1,0:T(8,128)} %bitcast.29, s32[8,128]{1,0:T(8,128)} %bitcast.31, f32[8,128]{1,0:T(8,128)} %bitcast.33, bf16[128,4096]{1,0:T(8,128)(2,1)} %tok.1), custom_call_target="tpu_custom_call" | custom-call | flops 2147483648 | bytes 8388608 | tf_op jit(solution)/shard_map/pallas_call | solution.py:92
  9.3 0.9 collective-permute-done.refs_1_.wg1
  10.1 0.0 copy-start
  10.1 1.1 collective-permute-done.1.refs_2_.wu1
  11.2 0.6 copy-done
  11.8 119.6 %all_to_all.10 = bf16[64,16,4736]{2,1,0:T(8,128)(2,1)} all-to-all(bf16[64,16,4736]{2,1,0:T(8,128)(2,1)} %bitcast.13), channel_id=1, replica_groups=mesh['exp'=64,'tp'=2] {'exp'}, dimensions={0} | all-to-all | bytes 19398656 | tf_op jit(solution)/shard_map/all_to_all | solution.py:366
  131.4 6.5 %shard_map.104 = (bf16[1024,512]{1,0:T(8,128)(2,1)}, f32[1152,128]{1,0:T(8,128)}, bf16[384,4096]{1,0:T(8,128)(2,1)}) custom-call(bf16[1024,4736]{1,0:T(8,128)(2,1)} %bitcast.14, bf16[1024,4736]{1,0:T(8,128)(2,1)} %bitcast.15, bf16[384,4096]{1,0:T(8,128)(2,1)} %bitcast.20), custom_call_target="tpu_custom_call" | custom-call | flops 1073741824 | bytes 2097152 | tf_op jit(solution)/shard_map/pallas_call | solution.py:127
  137.9 0.0 collective-permute-start.2
  137.9 23.0 %shard_map.105 = (bf16[1152,768]{1,0:T(8,128)(2,1)}, f32[1,5120]{1,0:T(1,128)}) custom-call(bf16[1024,4736]{1,0:T(8,128)(2,1)} %bitcast.16, bf16[1024,512]{1,0:T(8,128)(2,1)} %get-tuple-element.13.x_more, f32[1152,128]{1,0:T(8,128)} %get-tuple-element.14.w_col, bf16[4096,384]{1,0:T(8,128)(2,1)} %bitcast.24, bf16[4096,384]{1,0:T(8,128)(2,1)} %copy-done, ...), custom_call_target="tpu_custom_call" | custom-call | flops 14495514624 | bytes 20971520 | tf_op jit(solution)/shard_map/pallas_call | solution.py:192
  160.9 0.5 collective-permute-start.3
  161.4 0.0 collective-permute-done.2.wd1
  161.4 0.0 copy-start.2
  161.4 1.7 copy-done.2
  163.1 12.6 %shard_map.106.refs_0_ = bf16[1024,4608]{1,0:T(8,128)(2,1)} custom-call(bf16[1152,768]{1,0:T(8,128)(2,1)} %get-tuple-element.15.hid, bf16[384,4096]{1,0:T(8,128)(2,1)} %bitcast.21, bf16[384,4096]{1,0:T(8,128)(2,1)} %copy-done.2), custom_call_target="tpu_custom_call" | custom-call | flops 7247757312 | bytes 14680064 | tf_op jit(solution)/shard_map/pallas_call | solution.py:248
  175.7 0.0 collective-permute-done.3.refs_1_.other.other_hid
  175.7 0.0 copy-start.1
  175.7 0.6 copy-done.1
  176.3 116.1 %all_to_all.11 = bf16[64,16,4608]{2,1,0:T(8,128)(2,1)} all-to-all(bf16[64,16,4608]{2,1,0:T(8,128)(2,1)} %bitcast.19), channel_id=1, replica_groups=mesh['exp'=64,'tp'=2] {'exp'}, dimensions={0} | all-to-all | bytes 18874368 | tf_op jit(solution)/shard_map/all_to_all | solution.py:366
  292.4 12.5 %shard_map.108 = (bf16[128,4096]{1,0:T(8,128)(2,1)}, bf16[4096,384]{1,0:T(8,128)(2,1)}, bf16[4096,384]{1,0:T(8,128)(2,1)}, bf16[384,4096]{1,0:T(8,128)(2,1)}) custom-call(s32[8,128]{1,0:T(8,128)} %bitcast.30, s32[8,128]{1,0:T(8,128)} %bitcast.32, f32[8,128]{1,0:T(8,128)} %bitcast.34, bf16[1024,4608]{1,0:T(8,128)(2,1)} %bitcast.17, ...), custom_call_target="tpu_custom_call" | custom-call | flops 2147483648 | bytes 28311552 | tf_op jit(solution)/shard_map/pallas_call | solution.py:333
  (2 shorter events, 0.0 us)
Async XLA Ops:
  0.6 9.5 %collective-permute-start = (bf16[4096,384]{1,0:T(8,128)(2,1)}, bf16[4096,384]{1,0:T(8,128)(2,1)S(1)}, u32[]{:S(2)}, u32[]{:S(2)}) collective-permute-start(bf16[4096,384]{1,0:T(8,128)(2,1)} %bitcast.23), channel_id=1, source_target_pairs={{0,1},{1,0},{2,3},{3,2},{4,5},{5,4},{6,7},{7,6},{8,9},{9,8},{10,11... | collective-permute-start | bytes 9437192 | tf_op jit(solution)/shard_map/ppermute | solution.py:361
  0.7 10.5 %collective-permute-start.1 = (bf16[4096,384]{1,0:T(8,128)(2,1)}, bf16[4096,384]{1,0:T(8,128)(2,1)}, u32[]{:S(2)}, u32[]{:S(2)}) collective-permute-start(bf16[4096,384]{1,0:T(8,128)(2,1)} %bitcast.26), channel_id=1, source_target_pairs={{0,1},{1,0},{2,3},{3,2},{4,5},{5,4},{6,7},{7,6},{8,9},{9,8},{10,11... | collective-permute-start | bytes 9437192 | tf_op jit(solution)/shard_map/ppermute | solution.py:361
  10.1 1.7 copy-start
  137.9 23.5 %collective-permute-start.2 = (bf16[384,4096]{1,0:T(8,128)(2,1)}, bf16[384,4096]{1,0:T(8,128)(2,1)S(1)}, u32[]{:S(2)}, u32[]{:S(2)}) collective-permute-start(bf16[384,4096]{1,0:T(8,128)(2,1)} %get-tuple-element.16), channel_id=1, source_target_pairs={{0,1},{1,0},{2,3},{3,2},{4,5},{5,4},{6,7},{7,6},{8,9},{9,8},{10,11... | collective-permute-start | bytes 9437192 | tf_op jit(solution)/shard_map/ppermute | solution.py:361
  160.9 14.7 %collective-permute-start.3 = (f32[1,5120]{1,0:T(1,128)}, f32[1,5120]{1,0:T(1,128)S(1)}, u32[]{:S(2)}, u32[]{:S(2)}) collective-permute-start(f32[1,5120]{1,0:T(1,128)} %get-tuple-element.17.own.own_hid), channel_id=1, source_target_pairs={{0,1},{1,0},{2,3},{3,2},{4,5},{5,4},{6,7},{7,6},{8,9},{9,8},{10,11... | collective-permute-start | bytes 61448 | tf_op jit(solution)/shard_map/ppermute | solution.py:361
  161.4 1.7 copy-start.2
  175.7 0.6 copy-start.1

commit v3 on v1

v3 whole, which is shorter than its diff:
```python
import functools

import jax
import jax.numpy as jnp
from jax import lax
from jax.experimental import pallas as pl
from jax.experimental.pallas import tpu as pltpu
from jax.sharding import PartitionSpec as P

BF16, F32 = jnp.bfloat16, jnp.float32
CHUNK = 512
WIDE = 1024
HALVES = 2
EXTRA = 1
VMEM = 56 * 1024 * 1024


def iota(shape, dim):
    return lax.broadcasted_iota(jnp.int32, shape, dim)


def one_hot(match):
    return jnp.where(match, 1.0, 0.0).astype(BF16)


def params():
    return pltpu.CompilerParams(vmem_limit_bytes=VMEM)


def by_chunk(blocks, slots):
    more = blocks * EXTRA
    row = iota((blocks * slots, 1), 0)
    home = (row % more) // EXTRA * slots + row // more * EXTRA + row % EXTRA
    return one_hot(home == iota((blocks * slots, blocks * slots), 1))


def by_block(blocks, slots):
    more = blocks * EXTRA
    row = iota((blocks * slots, 1), 0)
    home = row % slots // EXTRA * more + row // slots * EXTRA + row % EXTRA
    return one_hot(home == iota((blocks * slots, blocks * slots), 1))


def assign(experts, routes, valid, probs):
    count = routes.shape[1]
    ids = iota((experts, count), 0)
    named, weight = jnp.zeros((experts, count), F32), jnp.zeros((experts, count), F32)
    for k in range(routes.shape[0]):
        hit = (routes[k : k + 1, :] == ids) & (valid[k : k + 1, :] > 0)
        named = named + jnp.where(hit, 1.0, 0.0)
        weight = weight + jnp.where(hit, probs[k : k + 1, :], 0.0)
    before = one_hot(iota((count, count), 0) < iota((count, count), 1))
    place = jnp.dot(named.astype(BF16), before, preferred_element_type=F32)
    return jnp.where(named > 0, place, -1.0).astype(jnp.int32), weight


def build_kernel(experts, slots, part, chunks, routes, valid, probs, tok, out, slot_scr, sel_scr, stack, w_scr):
    i = pl.program_id(0)
    count = routes.shape[1]
    rows = experts * slots
    row = iota((experts, slots, count), 1)

    @pl.when(i == 0)
    def _():
        slot, weight = assign(experts, routes, valid, probs)
        slot_scr[...] = slot
        slot, weight = slot.reshape(experts, 1, count), weight.reshape(experts, 1, count)
        first = part * (slots + EXTRA)
        sel_scr[...] = jnp.where(slot == row + first, 1.0, 0.0).reshape(rows, count).astype(BF16)
        if part == 0:
            lane = iota((experts, slots, 128), 2)
            packed = jnp.zeros((experts, slots, 128), F32)
            for h in range(HALVES):
                at = h * (slots + EXTRA)
                w_main = jnp.sum(jnp.where(slot == row + at, weight, 0.0), axis=2, keepdims=True)
                w_more = jnp.sum(
                    jnp.where((slot == row + (at + slots)) & (row < EXTRA), weight, 0.0), axis=2, keepdims=True
                )
                packed = jnp.where(lane == 2 * h, w_main, jnp.where(lane == 2 * h + 1, w_more, packed))
            w_scr[...] = packed.reshape(rows, 128).astype(BF16)

    @pl.when(i < chunks)
    def _():
        out[...] = jnp.dot(sel_scr[...], tok[...], preferred_element_type=F32).astype(BF16)
        for p in range(WIDE // CHUNK):
            at = pl.multiple_of((i * (WIDE // CHUNK) + p) * count, count)
            stack[pl.ds(at, count), :] = tok[:, p * CHUNK : (p + 1) * CHUNK]

    @pl.when(i == chunks)
    def _():
        slot = slot_scr[...].reshape(experts, 1, count)
        late = part * (slots + EXTRA) + slots
        wanted = jnp.where(slot == row % EXTRA + late, row // EXTRA, -1).reshape(rows, count)
        pick = jnp.concatenate([one_hot(wanted == c) for c in range(slots // EXTRA)], axis=1)
        out[:, 0:CHUNK] = jnp.dot(pick, stack[...], preferred_element_type=F32).astype(BF16)
        if part == 0:
            out[:, CHUNK : CHUNK + 128] = w_scr[...]


def build(part, routes, valid, probs, tokens, experts, slots):
    count, width = tokens.shape
    chunks = width // WIDE
    rows = experts * slots
    small = pl.BlockSpec((routes.shape[0], count), lambda i: (0, 0))
    return pl.pallas_call(
        functools.partial(build_kernel, experts, slots, part, chunks),
        grid=(chunks + 1,),
        in_specs=[small, small, small, pl.BlockSpec((count, WIDE), lambda i: (0, jnp.minimum(i, chunks - 1)))],
        out_specs=pl.BlockSpec((rows, WIDE), lambda i: (0, i)),
        out_shape=jax.ShapeDtypeStruct((rows, width + CHUNK + (128 if part == 0 else 0)), BF16),
        scratch_shapes=[
            pltpu.VMEM((experts, count), jnp.int32),
            pltpu.VMEM((rows, count), BF16),
            pltpu.VMEM((width // CHUNK * count, CHUNK), BF16),
            pltpu.VMEM((rows, 128), BF16),
        ],
        compiler_params=params(),
        cost_estimate=pl.CostEstimate(flops=4 * rows * count * width, bytes_accessed=2 * rows * width, transcendentals=0),
    )(routes, valid, probs, tokens)


def expert_kernel(blocks, slots, part, chunks, *refs):
    x, x_more, x_w, wg0, wg1, wu0, wu1, wd0, wd1 = refs[:9]
    so_far = refs[9] if part else None
    out, sq, more_scr, w_col, xs, acc0, acc1, hid = refs[10 if part else 9 :]
    i = pl.program_id(0)
    rows, more = blocks * slots, blocks * EXTRA
    half = wg0.shape[1]
    parts = WIDE // CHUNK
    base = lambda lanes: so_far[:, lanes] if part else 0.0

    @pl.when(i == 0)
    def _():
        acc0[...] = jnp.zeros_like(acc0)
        acc1[...] = jnp.zeros_like(acc1)
        pick = by_chunk(blocks, slots)
        more_scr[...] = jnp.dot(pick, x_more[...], preferred_element_type=F32).astype(BF16)
        lane = 2 * part
        w_main = x_w[...].astype(F32)
        w_more = jnp.dot(pick[0:more], x_w[...], preferred_element_type=F32)
        w_col[0:rows, :] = jnp.broadcast_to(w_main[:, lane : lane + 1], (rows, 128))
        w_col[rows : rows + more, :] = jnp.broadcast_to(w_more[:, lane + 1 : lane + 2], (more, 128))

    @pl.when(i < chunks)
    def _():
        xs[0:rows, :] = x[...]
        for p in range(parts):
            at = pl.multiple_of((i * parts + p) * more, more)
            xs[rows : rows + more, p * CHUNK : (p + 1) * CHUNK] = more_scr[pl.ds(at, more), :]
        acc0[...] += jnp.dot(xs[...], jnp.concatenate([wg0[...], wu0[...]], axis=1), preferred_element_type=F32)
        acc1[...] += jnp.dot(xs[...], jnp.concatenate([wg1[...], wu1[...]], axis=1), preferred_element_type=F32)
        for lane in range(0, WIDE, 128):
            lanes = slice(lane, lane + 128)
            value = xs[:, lanes].astype(F32)
            sq[:, lanes] = base(lanes) + jnp.sum(value * value * w_col[...], axis=0, keepdims=True)

    @pl.when(i == chunks)
    def _():
        sq[...] = jnp.zeros_like(sq)
        for at, acc in ((0, acc0), (half, acc1)):
            for lane in range(0, half, 128):
                gate = acc[:, lane : lane + 128]
                up = acc[:, half + lane : half + lane + 128]
                value = (gate / (1.0 + jnp.exp(-gate)) * up).astype(BF16)
                lanes = slice(at + lane, at + lane + 128)
                hid[:, lanes] = value
                value = value.astype(F32)
                sq[:, lanes] = base(lanes) + jnp.sum(value * value * w_col[...], axis=0, keepdims=True)

    @pl.when((i >= chunks) & (i < 2 * chunks))
    def _():
        result = jnp.dot(
            hid[...], jnp.concatenate([wd0[...], wd1[...]], axis=0), preferred_element_type=F32
        ).astype(BF16)
        out[...] = result[0:rows]
        for p in range(parts):
            at = pl.multiple_of(((i - chunks) * parts + p) * more, more)
            more_scr[pl.ds(at, more), :] = result[rows : rows + more, p * CHUNK : (p + 1) * CHUNK]

    @pl.when(i == 2 * chunks)
    def _():
        out[:, 0:CHUNK] = jnp.dot(
            by_block(blocks, slots), more_scr[...], preferred_element_type=F32
        ).astype(BF16)


def expert(part, received, carrier, weights, so_far, blocks, slots):
    width, half = weights[0].shape
    chunks = width // WIDE
    rows, more = blocks * slots, blocks * EXTRA
    up_to = lambda i: jnp.minimum(i, chunks - 1)
    after = lambda i: jnp.clip(i - chunks, 0, chunks - 1)
    w_in = pl.BlockSpec((WIDE, half), lambda i: (up_to(i), 0))
    w_out = pl.BlockSpec((half, WIDE), lambda i: (0, after(i)))
    sums = pl.BlockSpec((1, WIDE), lambda i: (0, jnp.minimum(i, chunks)))
    return pl.pallas_call(
        functools.partial(expert_kernel, blocks, slots, part, chunks),
        grid=(2 * chunks + 1,),
        in_specs=[
            pl.BlockSpec((rows, WIDE), lambda i: (0, up_to(i))),
            pl.BlockSpec((rows, CHUNK), lambda i: (0, width // CHUNK)),
            pl.BlockSpec((rows, 128), lambda i: (0, (width + CHUNK) // 128)),
            w_in, w_in, w_in, w_in, w_out, w_out,
        ] + [sums] * len(so_far),
        out_specs=[pl.BlockSpec((rows, WIDE), lambda i: (0, jnp.maximum(i - chunks, 0))), sums],
        out_shape=[
            jax.ShapeDtypeStruct((rows, width + CHUNK), BF16),
            jax.ShapeDtypeStruct((1, width + WIDE), F32),
        ],
        scratch_shapes=[
            pltpu.VMEM((rows, CHUNK), BF16),
            pltpu.VMEM((rows + more, 128), F32),
            pltpu.VMEM((rows + more, WIDE), BF16),
            pltpu.VMEM((rows + more, 2 * half), F32),
            pltpu.VMEM((rows + more, 2 * half), F32),
            pltpu.VMEM((rows + more, 2 * half), BF16),
        ],
        compiler_params=params(),
        cost_estimate=pl.CostEstimate(
            flops=12 * (rows + more) * width * half, bytes_accessed=4 * rows * width + 12 * width * half, transcendentals=0
        ),
    )(received, received, carrier, *weights, *so_far)


def column(line):
    eye = iota((128, 128), 0) == iota((128, 128), 1)
    return jnp.concatenate(
        [
            jnp.sum(jnp.where(eye, line[:, at : at + 128], 0.0), axis=1, keepdims=True)
            for at in range(0, line.shape[1], 128)
        ],
        axis=0,
    )


def combine_kernel(experts, slots, part, *refs):
    routes, valid, probs, x, x_more = refs[:5]
    if part:
        so_far, out, sel_scr, more_scr, stack = refs[5:]
    else:
        own, other, own_hid, other_hid, wg, wu, wd, out, s_gate, s_up, s_down, sel_scr, more_scr, stack = refs[5:]
    i = pl.program_id(0)
    count = routes.shape[1]
    rows, more = experts * slots, experts * EXTRA

    @pl.when(i == 0)
    def _():
        slot, weight = assign(experts, routes, valid, probs)
        slot, weight = slot.reshape(experts, 1, count), weight.reshape(experts, 1, count)
        first = part * (slots + EXTRA)
        hits = slot == iota((experts, slots, count), 1) + first
        sel_scr[...] = jnp.where(hits, weight, 0.0).reshape(rows, count).T.astype(BF16)
        spread = jnp.zeros((more, count), F32)
        for r in range(EXTRA):
            late = jnp.where(slot == first + slots + r, weight, 0.0).reshape(experts, count)
            widen = one_hot(iota((more, experts), 0) == iota((more, experts), 1) * EXTRA + r)
            spread = spread + jnp.dot(widen, late.astype(BF16), preferred_element_type=F32)
        more_scr[...] = spread.T.astype(BF16)
        stack[...] = jnp.dot(by_chunk(experts, slots), x_more[...], preferred_element_type=F32).astype(BF16)

    total = jnp.dot(sel_scr[...], x[...], preferred_element_type=F32)
    if part:
        total = total + so_far[...]
    for p in range(WIDE // CHUNK):
        at = pl.multiple_of((i * (WIDE // CHUNK) + p) * more, more)
        lanes = slice(p * CHUNK, (p + 1) * CHUNK)
        out[:, lanes] = (
            total[:, lanes] + jnp.dot(more_scr[...], stack[pl.ds(at, more), :], preferred_element_type=F32)
        ).astype(out.dtype)
    if not part:
        half = wg.shape[1]
        norm = column(jnp.sqrt(own[...] + other[...]))
        s_gate[...] = (jnp.abs(wg[...].astype(F32)) * norm).astype(BF16)
        s_up[...] = (jnp.abs(wu[...].astype(F32)) * norm).astype(BF16)
        norm = column(jnp.sqrt(own_hid[:, 0:half] + other_hid[:, half : 2 * half]))
        s_down[...] = (jnp.abs(wd[...].astype(F32)) * norm).astype(BF16)


def combine(part, routes, valid, probs, returned, experts, slots, so_far=None, own=None, other=None, weights=None):
    rows, wide = returned.shape
    width = wide - CHUNK
    chunks = width // WIDE
    count = routes.shape[1]
    small = pl.BlockSpec((routes.shape[0], count), lambda i: (0, 0))
    whole = pl.BlockSpec((count, WIDE), lambda i: (0, i))
    in_specs = [
        small, small, small,
        pl.BlockSpec((rows, WIDE), lambda i: (0, i)),
        pl.BlockSpec((rows, CHUNK), lambda i: (0, width // CHUNK)),
    ]
    if part:
        in_specs, out_specs = in_specs + [whole], whole
        out_shape = jax.ShapeDtypeStruct((count, width), BF16)
        given = (so_far,)
    else:
        half = weights[0].shape[1]
        tall = pl.BlockSpec((WIDE, half), lambda i: (i, 0))
        flat = pl.BlockSpec((half, WIDE), lambda i: (0, i))
        sums = pl.BlockSpec((1, WIDE), lambda i: (0, i))
        last = pl.BlockSpec((1, WIDE), lambda i: (0, chunks))
        in_specs = in_specs + [sums, sums, last, last, tall, tall, flat]
        out_specs = [whole, tall, tall, flat]
        out_shape = [jax.ShapeDtypeStruct((count, width), F32)] + [jax.ShapeDtypeStruct(w.shape, BF16) for w in weights]
        given = (own, other, own, other) + tuple(weights)
    return pl.pallas_call(
        functools.partial(combine_kernel, experts, slots, part),
        grid=(chunks,),
        in_specs=in_specs,
        out_specs=out_specs,
        out_shape=out_shape,
        scratch_shapes=[
            pltpu.VMEM((count, rows), BF16),
            pltpu.VMEM((count, experts * EXTRA), BF16),
            pltpu.VMEM((rows, CHUNK), BF16),
        ],
        compiler_params=params(),
        cost_estimate=pl.CostEstimate(flops=4 * rows * count * width, bytes_accessed=6 * rows * wide, transcendentals=0),
    )(routes, valid, probs, returned, returned, *given)


def swap(value):
    return lax.ppermute(value, "tp", [(0, 1), (1, 0)])


def exchange(value, experts, slots):
    value = value.reshape(experts, slots, value.shape[1])
    value = lax.all_to_all(value, "exp", split_axis=0, concat_axis=0, tiled=True)
    return value.reshape(experts * slots, value.shape[2])


def per_device(tokens, gate_weight, up_weight, down_weight, routes, gate_probs, valid_mask):
    count, top = routes.shape
    experts = lax.axis_size("exp")
    cap = max(2, count * top * 9 // (8 * experts))
    slots = cap // HALVES - EXTRA
    own = gate_weight[0], up_weight[0], down_weight[0]
    weights = [w for mine in own for w in (mine, swap(mine))]
    routing = routes.T, valid_mask.T, gate_probs.T
    sent = [build(part, *routing, tokens, experts, slots) for part in range(HALVES)]
    received = [exchange(half, experts, slots) for half in sent]
    outs0, sums = expert(0, received[0], received[0], weights, (), experts, slots)
    outs1, sums = expert(1, received[1], received[0], weights, (sums,), experts, slots)
    returned = [exchange(half, experts, slots) for half in (outs0, outs1)]
    mixed, score_gate, score_up, score_down = combine(
        0, *routing, returned[0], experts, slots, own=sums, other=swap(sums), weights=own
    )
    mixed = combine(1, *routing, returned[1], experts, slots, so_far=mixed)
    return (mixed, score_gate[None], score_up[None], score_down[None])


def solution(mesh):
    in_specs = (
        P(("exp", "tp"), None),
        P("exp", None, "tp"),
        P("exp", None, "tp"),
        P("exp", "tp", None),
        P(("exp", "tp"), None),
        P(("exp", "tp"), None),
        P(("exp", "tp"), None),
    )
    out_specs = (
        P(("exp", "tp"), None),
        P("exp", None, "tp"),
        P("exp", None, "tp"),
        P("exp", "tp", None),
    )
    return jax.shard_map(
        per_device, mesh=mesh, in_specs=in_specs, out_specs=out_specs, check_vma=False
    )
```

time: 370 us -> 306 us (0.83)
  waiting for transfers between devices: 272 us -> 191 us
  starting transfers between devices: 25.8 us -> 43 us
  Pallas kernels: 57.3 us -> 69 us
  other arithmetic: 6.07 us -> 0 us
    all_to_all x2 -> x4, waiting for transfers between devices: 256 us -> 175 us  [exchange(): lax.all_to_all(value, 'exp', split_axis=0, concat_axis=0, tiled=True)]
    all_to_all x2 -> x4, starting transfers between devices: 24.8 us -> 42.2 us  [exchange(): lax.all_to_all(value, 'exp', split_axis=0, concat_axis=0, tiled=True)]
    pallas_call x3 -> x6, Pallas kernels: 57.3 us -> 69 us  [the longest x2 40.2 us: expert(): pl.pallas_call(functools.partial(expert_kernel, blocks, slots, part, chun...]
    convert_element_type x2 -> x0, other arithmetic: 6.06 us -> none  [the longest x1 3.5 us: per_device(): score_up = (jnp.abs(w_up.astype(F32)) * in_norm).astype(BF16)]
  transfers between devices with their start and end apart: 6 -> 8, of which waited for: 5 -> 8; matrix products, arithmetic and copies ran while one was open for 2% -> 0% of each run, Pallas kernels for 0% -> 19%
where the time goes in v3:
time: 306 us; the launch traced here: 304 us
  waiting for transfers between devices  191 us (62%)
  Pallas kernels  69 us (23%)
  starting transfers between devices  43 us (14%)
    all_to_all x4, waiting for transfers between devices, exchange(): lax.all_to_all(value, 'exp', split_axis=0, concat_axis=0, tiled=True)  175 us
    all_to_all x4, starting transfers between devices, exchange(): lax.all_to_all(value, 'exp', split_axis=0, concat_axis=0, tiled=True)  42.2 us
    pallas_call x2, Pallas kernels, expert(): pl.pallas_call(functools.partial(expert_kernel, blocks, slots, part, chun...  40.2 us
    pallas_call x2, Pallas kernels, combine(): pl.pallas_call(functools.partial(combine_kernel, experts, slots, part), g...  16.8 us
    ppermute x4, waiting for transfers between devices, swap(): return lax.ppermute(value, 'tp', [(0, 1), (1, 0)])  15.6 us
    pallas_call x2, Pallas kernels, build(): pl.pallas_call(functools.partial(build_kernel, experts, slots, part, chun...  12 us
  transfers between devices with their start and end apart: 8, of which 8 were waited for; matrix products, arithmetic and copies ran while one was open for 0% of the time, Pallas kernels for 19%

profile of v3, /device:TPU:50, one launch (start us, length us, event | category | flops | bytes accessed | tf_op | source)
XLA Modules:
  0.0 304.1 jit_solution(10310674137739894022)
XLA Ops:
  0.6 6.2 %shard_map.103 = bf16[512,4736]{1,0:T(8,128)(2,1)} custom-call(s32[8,128]{1,0:T(8,128)} %bitcast.33, s32[8,128]{1,0:T(8,128)} %bitcast.37, f32[8,128]{1,0:T(8,128)} %bitcast.41, bf16[128,4096]{1,0:T(8,128)(2,1)} %tok.3), custom_call_target="tpu_custom_call" | custom-call | flops 1073741824 | bytes 4194304 | tf_op jit(solution)/shard_map/pallas_call | solution.py:105
  6.8 11.0 %all-to-all-start.1 = ((bf16[64,8,4736]{2,1,0:T(8,128)(2,1)}), bf16[64,8,4736]{2,1,0:T(8,128)(2,1)}, u32[]{:S(2)}, u32[]{:S(2)}) async-start(bf16[64,8,4736]{2,1,0:T(8,128)(2,1)} %bitcast.17), calls=%async_computation.1 | async-start | bytes 9699328 | tf_op jit(solution)/shard_map/all_to_all | solution.py:327
  17.8 5.8 %shard_map.102 = bf16[512,4608]{1,0:T(8,128)(2,1)} custom-call(s32[8,128]{1,0:T(8,128)} %bitcast.34, s32[8,128]{1,0:T(8,128)} %bitcast.38, f32[8,128]{1,0:T(8,128)} %bitcast.42, bf16[128,4096]{1,0:T(8,128)(2,1)} %tok.3), custom_call_target="tpu_custom_call" | custom-call | flops 1073741824 | bytes 4194304 | tf_op jit(solution)/shard_map/pallas_call | solution.py:105
  23.6 60.8 %all-to-all-done.1 = bf16[64,8,4736]{2,1,0:T(8,128)(2,1)} async-done(((bf16[64,8,4736]{2,1,0:T(8,128)(2,1)}), bf16[64,8,4736]{2,1,0:T(8,128)(2,1)}, u32[]{:S(2)}, u32[]{:S(2)}) %all-to-all-start.1) | async-done | bytes 4849696 | tf_op jit(solution)/shard_map/all_to_all | solution.py:327
  84.4 0.0 copy-start
  84.4 10.0 %all-to-all-start = ((bf16[64,8,4608]{2,1,0:T(8,128)(2,1)}), bf16[64,8,4608]{2,1,0:T(8,128)(2,1)}, u32[]{:S(2)}, u32[]{:S(2)}) async-start(bf16[64,8,4608]{2,1,0:T(8,128)(2,1)} %bitcast.18), calls=%async_computation | async-start | bytes 9437184 | tf_op jit(solution)/shard_map/all_to_all | solution.py:327
  94.4 0.0 copy-done
  94.4 0.1 collective-permute-start
  94.5 0.5 collective-permute-start.1
  95.0 0.1 collective-permute-start.2
  95.1 8.6 %collective-permute-done.refs_4_ = bf16[4096,384]{1,0:T(8,128)(2,1)S(1)} collective-permute-done((bf16[4096,384]{1,0:T(8,128)(2,1)S(1)}, bf16[4096,384]{1,0:T(8,128)(2,1)S(1)}, u32[]{:S(2)}, u32[]{:S(2)}) %collective-permute-start) | collective-permute-done | bytes 3145760 | tf_op jit(solution)/shard_map/ppermute | solution.py:322
  103.7 0.0 copy-start.3
  103.7 1.3 collective-permute-done.1.refs_6_
  105.0 4.5 %collective-permute-done.2.refs_8_ = bf16[384,4096]{1,0:T(8,128)(2,1)} collective-permute-done((bf16[384,4096]{1,0:T(8,128)(2,1)}, bf16[384,4096]{1,0:T(8,128)(2,1)}, u32[]{:S(2)}, u32[]{:S(2)}) %collective-permute-start.2) | collective-permute-done | bytes 3145760 | tf_op jit(solution)/shard_map/ppermute | solution.py:322
  109.5 0.0 copy-done.3
  109.5 20.1 %shard_map.104 = (bf16[512,4608]{1,0:T(8,128)(2,1)}, f32[1,5120]{1,0:T(1,128)}) custom-call(bf16[512,4736]{1,0:T(8,128)(2,1)} %bitcast.6.refs_0_.refs_1_.refs_2_, bf16[512,4736]{1,0:T(8,128)(2,1)} %bitcast.6.refs_0_.refs_1_.refs_2_, bf16[512,4736]{1,0:T(8,128)(2,1)} %bitcast.6.refs_0_.refs_1_.refs_2_, bf16[4096,384]{1,0:T(8,128)(2,1)} %bitcast.21, ...), custom_call_target="tpu_custom_call" | custom-call | flops 10871635968 | bytes 27262976 | tf_op jit(solution)/shard_map/pallas_call | solution.py:196
  129.6 23.0 %all-to-all-done = bf16[64,8,4608]{2,1,0:T(8,128)(2,1)} async-done(((bf16[64,8,4608]{2,1,0:T(8,128)(2,1)}), bf16[64,8,4608]{2,1,0:T(8,128)(2,1)}, u32[]{:S(2)}, u32[]{:S(2)}) %all-to-all-start) | async-done | bytes 4718624 | tf_op jit(solution)/shard_map/all_to_all | solution.py:327
  152.6 11.6 %all-to-all-start.3 = ((bf16[64,8,4608]{2,1,0:T(8,128)(2,1)}), bf16[64,8,4608]{2,1,0:T(8,128)(2,1)}, u32[]{:S(2)}, u32[]{:S(2)}) async-start(bf16[64,8,4608]{2,1,0:T(8,128)(2,1)} %bitcast.20), calls=%async_computation.3 | async-start | bytes 9437184 | tf_op jit(solution)/shard_map/all_to_all | solution.py:327
  164.1 20.1 %shard_map.105 = (bf16[512,4608]{1,0:T(8,128)(2,1)}, f32[1,5120]{1,0:T(1,128)}) custom-call(bf16[512,4608]{1,0:T(8,128)(2,1)} %bitcast.4.refs_0_.refs_1_, bf16[512,4608]{1,0:T(8,128)(2,1)} %bitcast.4.refs_0_.refs_1_, bf16[512,4736]{1,0:T(8,128)(2,1)} %bitcast.6.refs_0_.refs_1_.refs_2_, bf16[4096,384]{1,0:T(8,128)(2,1)} %bitcast.22, ...), custom_call_target="tpu_custom_call" | custom-call | flops 10871635968 | bytes 27262976 | tf_op jit(solution)/shard_map/pallas_call | solution.py:196
  184.3 44.9 %all-to-all-done.3 = bf16[64,8,4608]{2,1,0:T(8,128)(2,1)} async-done(((bf16[64,8,4608]{2,1,0:T(8,128)(2,1)}), bf16[64,8,4608]{2,1,0:T(8,128)(2,1)}, u32[]{:S(2)}, u32[]{:S(2)}) %all-to-all-start.3) | async-done | bytes 4718624 | tf_op jit(solution)/shard_map/all_to_all | solution.py:327
  229.1 0.0 copy-start.1
  229.2 9.6 %all-to-all-start.2 = ((bf16[64,8,4608]{2,1,0:T(8,128)(2,1)}), bf16[64,8,4608]{2,1,0:T(8,128)(2,1)}, u32[]{:S(2)}, u32[]{:S(2)}) async-start(bf16[64,8,4608]{2,1,0:T(8,128)(2,1)} %bitcast.19), calls=%async_computation.2 | async-start | bytes 9437184 | tf_op jit(solution)/shard_map/all_to_all | solution.py:327
  238.8 0.0 copy-done.1
  238.8 0.1 collective-permute-start.3
  238.9 1.2 collective-permute-done.3.refs_6_.refs_8_
  240.1 0.0 copy-start.2
  240.1 0.6 copy-done.2
  240.7 10.9 %shard_map.106 = (f32[128,4096]{1,0:T(8,128)}, bf16[4096,384]{1,0:T(8,128)(2,1)}, bf16[4096,384]{1,0:T(8,128)(2,1)}, bf16[384,4096]{1,0:T(8,128)(2,1)}) custom-call(s32[8,128]{1,0:T(8,128)} %bitcast.35, s32[8,128]{1,0:T(8,128)} %bitcast.39, f32[8,128]{1,0:T(8,128)} %bitcast.43, bf16[512,4608]{1,0:T(8,128)(2,1)} %bitcast.13.refs_3_.refs_4_, ...), custom_call_target="tpu_custom_call" | custom-call | flops 1073741824 | bytes 14155776 | tf_op jit(solution)/shard_map/pallas_call | solution.py:305
  251.6 46.6 %all-to-all-done.2 = bf16[64,8,4608]{2,1,0:T(8,128)(2,1)} async-done(((bf16[64,8,4608]{2,1,0:T(8,128)(2,1)}), bf16[64,8,4608]{2,1,0:T(8,128)(2,1)}, u32[]{:S(2)}, u32[]{:S(2)}) %all-to-all-start.2) | async-done | bytes 4718624 | tf_op jit(solution)/shard_map/all_to_all | solution.py:327
  298.2 5.9 %shard_map.107 = bf16[128,4096]{1,0:T(8,128)(2,1)} custom-call(s32[8,128]{1,0:T(8,128)} %bitcast.36, s32[8,128]{1,0:T(8,128)} %bitcast.40, f32[8,128]{1,0:T(8,128)} %bitcast.44, bf16[512,4608]{1,0:T(8,128)(2,1)} %bitcast.11.refs_3_.refs_4_, bf16[512,4608]{1,0:T(8,128)(2,1)} %bitcast.11.refs_3_.refs_4_, f32[128,4096]{1,0:T(8,128)} %get-tuple-element.16.refs_5_), custom_call_target="tpu_custom_call" | custom-call | flops 1073741824 | bytes 14155776 | tf_op jit(solution)/shard_map/pallas_call | solution.py:305
Async XLA Ops:
  6.8 77.6 %all-to-all-start.1 = ((bf16[64,8,4736]{2,1,0:T(8,128)(2,1)}), bf16[64,8,4736]{2,1,0:T(8,128)(2,1)}, u32[]{:S(2)}, u32[]{:S(2)}) async-start(bf16[64,8,4736]{2,1,0:T(8,128)(2,1)} %bitcast.17), calls=%async_computation.1 | async-start | bytes 9699328 | tf_op jit(solution)/shard_map/all_to_all | solution.py:327
  84.4 10.0 %copy-start = (bf16[1,4096,384]{2,1,0:T(8,128)(2,1)S(1)}, bf16[1,4096,384]{2,1,0:T(8,128)(2,1)}, u32[]{:S(2)}) copy-start(bf16[1,4096,384]{2,1,0:T(8,128)(2,1)} %param.8) | copy-start | bytes 9437188
  84.4 68.2 %all-to-all-start = ((bf16[64,8,4608]{2,1,0:T(8,128)(2,1)}), bf16[64,8,4608]{2,1,0:T(8,128)(2,1)}, u32[]{:S(2)}, u32[]{:S(2)}) async-start(bf16[64,8,4608]{2,1,0:T(8,128)(2,1)} %bitcast.18), calls=%async_computation | async-start | bytes 9437184 | tf_op jit(solution)/shard_map/all_to_all | solution.py:327
  94.4 9.3 %collective-permute-start = (bf16[4096,384]{1,0:T(8,128)(2,1)S(1)}, bf16[4096,384]{1,0:T(8,128)(2,1)S(1)}, u32[]{:S(2)}, u32[]{:S(2)}) collective-permute-start(bf16[4096,384]{1,0:T(8,128)(2,1)S(1)} %bitcast.24), channel_id=1, source_target_pairs={{0,1},{1,0},{2,3},{3,2},{4,5},{5,4},{6,7},{7,6},{8,9},{9,8},{10,11... | collective-permute-start | bytes 9437192 | tf_op jit(solution)/shard_map/ppermute | solution.py:322
  94.5 10.5 %collective-permute-start.1 = (bf16[4096,384]{1,0:T(8,128)(2,1)}, bf16[4096,384]{1,0:T(8,128)(2,1)}, u32[]{:S(2)}, u32[]{:S(2)}) collective-permute-start(bf16[4096,384]{1,0:T(8,128)(2,1)} %bitcast.25), channel_id=1, source_target_pairs={{0,1},{1,0},{2,3},{3,2},{4,5},{5,4},{6,7},{7,6},{8,9},{9,8},{10,11... | collective-permute-start | bytes 9437192 | tf_op jit(solution)/shard_map/ppermute | solution.py:322
  95.0 14.5 %collective-permute-start.2 = (bf16[384,4096]{1,0:T(8,128)(2,1)}, bf16[384,4096]{1,0:T(8,128)(2,1)}, u32[]{:S(2)}, u32[]{:S(2)}) collective-permute-start(bf16[384,4096]{1,0:T(8,128)(2,1)} %bitcast.29), channel_id=1, source_target_pairs={{0,1},{1,0},{2,3},{3,2},{4,5},{5,4},{6,7},{7,6},{8,9},{9,8},{10,11... | collective-permute-start | bytes 9437192 | tf_op jit(solution)/shard_map/ppermute | solution.py:322
  103.7 5.8 %copy-start.3 = (bf16[4096,384]{1,0:T(8,128)(2,1)}, bf16[4096,384]{1,0:T(8,128)(2,1)S(1)}, u32[]{:S(2)}) copy-start(bf16[4096,384]{1,0:T(8,128)(2,1)S(1)} %collective-permute-done.refs_4_) | copy-start | bytes 9437188
  152.6 76.6 %all-to-all-start.3 = ((bf16[64,8,4608]{2,1,0:T(8,128)(2,1)}), bf16[64,8,4608]{2,1,0:T(8,128)(2,1)}, u32[]{:S(2)}, u32[]{:S(2)}) async-start(bf16[64,8,4608]{2,1,0:T(8,128)(2,1)} %bitcast.20), calls=%async_computation.3 | async-start | bytes 9437184 | tf_op jit(solution)/shard_map/all_to_all | solution.py:327
  229.1 9.6 %copy-start.1 = (f32[1,5120]{1,0:T(1,128)S(1)}, f32[1,5120]{1,0:T(1,128)}, u32[]{:S(2)}) copy-start(f32[1,5120]{1,0:T(1,128)} %get-tuple-element.15.refs_5_.refs_7_) | copy-start | bytes 61444
  229.2 69.1 %all-to-all-start.2 = ((bf16[64,8,4608]{2,1,0:T(8,128)(2,1)}), bf16[64,8,4608]{2,1,0:T(8,128)(2,1)}, u32[]{:S(2)}, u32[]{:S(2)}) async-start(bf16[64,8,4608]{2,1,0:T(8,128)(2,1)} %bitcast.19), calls=%async_computation.2 | async-start | bytes 9437184 | tf_op jit(solution)/shard_map/all_to_all | solution.py:327
  238.8 1.3 collective-permute-start.3
  240.1 0.6 copy-start.2

commit v4 on v2

v4 whole, which is shorter than its diff:
```python
import functools

import jax
import jax.numpy as jnp
from jax import lax
from jax.experimental import pallas as pl
from jax.experimental.pallas import tpu as pltpu
from jax.sharding import PartitionSpec as P

BF16, F32 = jnp.bfloat16, jnp.float32
CHUNK = 512
WIDE = 1024
PIECES = 3
VMEM = 56 * 1024 * 1024


def iota(shape, dim):
    return lax.broadcasted_iota(jnp.int32, shape, dim)


def one_hot(match):
    return jnp.where(match, 1.0, 0.0).astype(BF16)


def planes(width):
    return [(plane, slice(plane * 128, (plane + 1) * 128)) for plane in range(width // 128)]


def to_chunks(wide, packed, by_chunk, blocks, slots):
    for plane, lanes in planes(CHUNK):
        wide[plane] = packed[:, lanes].astype(F32)
        for at in range(slots):
            picked = wide[plane, pl.ds(at, blocks, stride=slots), :]
            by_chunk[at * blocks : (at + 1) * blocks, lanes] = picked.astype(BF16)


def to_blocks(wide, by_chunk, packed, blocks, slots):
    for plane, lanes in planes(CHUNK):
        for at in range(slots):
            rows = by_chunk[at * blocks : (at + 1) * blocks, lanes]
            wide[plane, pl.ds(at, blocks, stride=slots), :] = rows.astype(F32)
        packed[:, lanes] = wide[plane].astype(BF16)


def assign(experts, routes, valid, probs):
    count = routes.shape[1]
    ids = iota((experts, count), 0)
    named, weight = jnp.zeros((experts, count), F32), jnp.zeros((experts, count), F32)
    for k in range(routes.shape[0]):
        hit = (routes[k : k + 1, :] == ids) & (valid[k : k + 1, :] > 0)
        named = named + jnp.where(hit, 1.0, 0.0)
        weight = weight + jnp.where(hit, probs[k : k + 1, :], 0.0)
    before = one_hot(iota((count, count), 0) < iota((count, count), 1))
    place = jnp.dot(named.astype(BF16), before, preferred_element_type=F32)
    return jnp.where(named > 0, place, -1.0).astype(jnp.int32), weight


def build_kernel(experts, slots, extra, chunks, routes, valid, probs, tok, out, back, back_more, sel_scr, pick_scr, stack, wide, w_scr):
    i = pl.program_id(0)
    more = experts * extra
    count = routes.shape[1]
    rows = experts * slots
    row = iota((experts, slots, count), 1)

    @pl.when(i == 0)
    def _():
        slot, weight = assign(experts, routes, valid, probs)
        slot, weight = slot.reshape(experts, 1, count), weight.reshape(experts, 1, count)
        hits = slot == row
        sel_scr[...] = jnp.where(hits, 1.0, 0.0).reshape(rows, count).astype(BF16)
        w_main = jnp.sum(jnp.where(hits, weight, 0.0), axis=2, keepdims=True)
        w_more = jnp.sum(jnp.where((slot == row + slots) & (row < extra), weight, 0.0), axis=2, keepdims=True)
        lane = iota((experts, slots, 128), 2)
        packed = jnp.where(lane == 0, w_main, jnp.where(lane == 1, w_more, 0.0))
        w_scr[...] = packed.reshape(rows, 128).astype(BF16)
        back[...] = jnp.where(hits, weight, 0.0).reshape(rows, count).T.astype(BF16)
        for r in range(extra):
            late = (slot == slots + r).reshape(experts, count)
            pick_scr[r * experts : (r + 1) * experts, :] = jnp.where(late, 1.0, 0.0).astype(BF16)
        late = [jnp.where(slot == slots + r, weight, 0.0).reshape(experts, count) for r in range(extra)]
        back_more[...] = jnp.concatenate(late, axis=0).T.astype(BF16)

    @pl.when(i < chunks)
    def _():
        out[...] = jnp.dot(sel_scr[...], tok[...], preferred_element_type=F32).astype(BF16)
        late = jnp.dot(pick_scr[...], tok[...], preferred_element_type=F32).astype(BF16)
        for part in range(WIDE // CHUNK):
            at = pl.multiple_of((i * (WIDE // CHUNK) + part) * more, more)
            stack[pl.ds(at, more), :] = late[:, part * CHUNK : (part + 1) * CHUNK]

    @pl.when(i == chunks)
    def _():
        to_blocks(wide, stack, out, experts, slots)
        out[:, CHUNK : CHUNK + 128] = w_scr[...]


def build(routes, valid, probs, tokens, experts, slots, extra):
    count, width = tokens.shape
    chunks = width // WIDE
    rows = experts * slots
    small = pl.BlockSpec((routes.shape[0], count), lambda i: (0, 0))
    return pl.pallas_call(
        functools.partial(build_kernel, experts, slots, extra, chunks),
        grid=(chunks + 1,),
        in_specs=[small, small, small, pl.BlockSpec((count, WIDE), lambda i: (0, jnp.minimum(i, chunks - 1)))],
        out_specs=[
            pl.BlockSpec((rows, WIDE), lambda i: (0, i)),
            pl.BlockSpec((count, rows), lambda i: (0, 0)),
            pl.BlockSpec((count, experts * extra), lambda i: (0, 0)),
        ],
        out_shape=[
            jax.ShapeDtypeStruct((rows, width + CHUNK + 128), BF16),
            jax.ShapeDtypeStruct((count, rows), BF16),
            jax.ShapeDtypeStruct((count, experts * extra), BF16),
        ],
        scratch_shapes=[
            pltpu.VMEM((rows, count), BF16),
            pltpu.VMEM((experts * extra, count), BF16),
            pltpu.VMEM((rows, CHUNK), BF16),
            pltpu.VMEM((CHUNK // 128, rows, 128), F32),
            pltpu.VMEM((rows, 128), BF16),
        ],
        compiler_params=pltpu.CompilerParams(vmem_limit_bytes=VMEM),
        cost_estimate=pl.CostEstimate(flops=4 * rows * count * width, bytes_accessed=2 * rows * width, transcendentals=0),
    )(routes, valid, probs, tokens)


def copy_kernel(given, first, copied, held, sem_in, sem_out):
    count = held.shape[0]
    pieces = [pl.ds(at * WIDE, WIDE) for at in range(count)]
    ins = [pltpu.make_async_copy(given.at[:, p], held.at[at], sem_in.at[at]) for at, p in enumerate(pieces)]
    outs = [pltpu.make_async_copy(held.at[at], copied.at[:, p], sem_out.at[at]) for at, p in enumerate(pieces)]
    for copy in ins:
        copy.start()
    for at in range(count):
        ins[at].wait()
        outs[at].start()
    for copy in outs:
        copy.wait()


def copy_after(value, first):
    high, width = value.shape
    count = width // WIDE
    anywhere = pl.BlockSpec(memory_space=pl.ANY)
    return pl.pallas_call(
        copy_kernel,
        in_specs=[anywhere, anywhere],
        out_specs=anywhere,
        out_shape=jax.ShapeDtypeStruct(value.shape, value.dtype),
        scratch_shapes=[
            pltpu.VMEM((count, high, WIDE), value.dtype),
            pltpu.SemaphoreType.DMA((count,)),
            pltpu.SemaphoreType.DMA((count,)),
        ],
        compiler_params=pltpu.CompilerParams(vmem_limit_bytes=VMEM),
        cost_estimate=pl.CostEstimate(flops=0, bytes_accessed=4 * high * width, transcendentals=0),
    )(value, first)


def hidden_kernel(blocks, slots, extra, chunks, x, x_more, x_w, wg0, wg1, wu0, wu1, hid, sq, xs, acc0, acc1, w_col,
                  wide, late):
    i = pl.program_id(0)
    rows, more = blocks * slots, blocks * extra
    half = wg0.shape[1]
    parts = WIDE // CHUNK

    def fill():
        xs[0:rows, :] = x[...]
        for part in range(parts):
            at = pl.multiple_of((i * parts + part) * more, more)
            xs[rows : rows + more, part * CHUNK : (part + 1) * CHUNK] = late[pl.ds(at, more), :]

    def squares():
        for lane in range(0, WIDE, 128):
            part = xs[:, lane : lane + 128].astype(F32)
            sq[:, lane : lane + 128] = jnp.sum(part * part * w_col[...], axis=0, keepdims=True)

    def products(at, high):
        piece = xs[at : at + high, :]
        return (
            jnp.dot(piece, jnp.concatenate([wg0[...], wu0[...]], axis=1), preferred_element_type=F32),
            jnp.dot(piece, jnp.concatenate([wg1[...], wu1[...]], axis=1), preferred_element_type=F32),
        )

    @pl.when(i == 0)
    def _():
        wide[0] = x_w[...].astype(F32)
        w_col[0:rows, :] = jnp.broadcast_to(wide[0, :, 0:1], (rows, 128))
        for r in range(extra):
            w_more = wide[0, pl.ds(r, blocks, stride=slots), :]
            w_col[rows + r * blocks : rows + (r + 1) * blocks, :] = jnp.broadcast_to(w_more[:, 1:2], (blocks, 128))
        to_chunks(wide, x_more, late, blocks, slots)
        fill()
        acc0[...], acc1[...] = products(0, rows + more)
        squares()

    @pl.when((i > 0) & (i < chunks - 1))
    def _():
        fill()
        first, second = products(0, rows + more)
        acc0[...] += first
        acc1[...] += second
        squares()

    @pl.when(i == chunks - 1)
    def _():
        fill()
        squares()
        high = (rows + more) // PIECES
        for at in range(0, rows + more, high):
            span = slice(at, at + high)
            for start, acc, product in zip((0, half), (acc0, acc1), products(at, high)):
                gate = acc[span, 0:half] + product[:, 0:half]
                up = acc[span, half : 2 * half] + product[:, half : 2 * half]
                hid[span, start : start + half] = (gate * (0.5 + 0.5 * jnp.tanh(0.5 * gate)) * up).astype(BF16)

    @pl.when(i == chunks)
    def _():
        sq[...] = jnp.zeros_like(sq)
        for lane in range(0, 2 * half, 128):
            value = hid[:, lane : lane + 128].astype(F32)
            sq[:, lane : lane + 128] = jnp.sum(value * value * w_col[...], axis=0, keepdims=True)


def hidden_units(received, wg0, wg1, wu0, wu1, blocks, slots, extra):
    width, half = wg0.shape
    chunks = width // WIDE
    rows, more = blocks * slots, blocks * extra
    up_to = lambda i: jnp.minimum(i, chunks - 1)
    w_in = pl.BlockSpec((WIDE, half), lambda i: (up_to(i), 0))
    return pl.pallas_call(
        functools.partial(hidden_kernel, blocks, slots, extra, chunks),
        grid=(chunks + 1,),
        in_specs=[
            pl.BlockSpec((rows, WIDE), lambda i: (0, up_to(i))),
            pl.BlockSpec((rows, CHUNK), lambda i: (0, width // CHUNK)),
            pl.BlockSpec((rows, 128), lambda i: (0, (width + CHUNK) // 128)),
            w_in, w_in, w_in, w_in,
        ],
        out_specs=[
            pl.BlockSpec((rows + more, 2 * half), lambda i: (0, 0)),
            pl.BlockSpec((1, WIDE), lambda i: (0, i)),
        ],
        out_shape=[
            jax.ShapeDtypeStruct((rows + more, 2 * half), BF16),
            jax.ShapeDtypeStruct((1, width + WIDE), F32),
        ],
        scratch_shapes=[
            pltpu.VMEM((rows + more, WIDE), BF16),
            pltpu.VMEM((rows + more, 2 * half), F32),
            pltpu.VMEM((rows + more, 2 * half), F32),
            pltpu.VMEM((rows + more, 128), F32),
            pltpu.VMEM((CHUNK // 128, rows, 128), F32),
            pltpu.VMEM((rows, CHUNK), BF16),
        ],
        compiler_params=pltpu.CompilerParams(vmem_limit_bytes=VMEM),
        cost_estimate=pl.CostEstimate(
            flops=8 * (rows + more) * width * half, bytes_accessed=2 * rows * width + 8 * width * half, transcendentals=0
        ),
    )(received, received, received, wg0, wg1, wu0, wu1)


def down_kernel(blocks, slots, extra, chunks, hid, wd0, wd1, out, stack, wide):
    i = pl.program_id(0)
    rows, more = blocks * slots, blocks * extra
    parts = WIDE // CHUNK

    @pl.when(i < chunks)
    def _():
        result = jnp.dot(
            hid[...], jnp.concatenate([wd0[...], wd1[...]], axis=0), preferred_element_type=F32
        ).astype(BF16)
        out[...] = result[0:rows]
        for part in range(parts):
            at = pl.multiple_of((i * parts + part) * more, more)
            stack[pl.ds(at, more), :] = result[rows : rows + more, part * CHUNK : (part + 1) * CHUNK]

    @pl.when(i == chunks)
    def _():
        to_blocks(wide, stack, out, blocks, slots)


def down(hid, wd0, wd1, blocks, slots, extra):
    half, width = wd0.shape
    chunks = width // WIDE
    rows = blocks * slots
    w_out = pl.BlockSpec((half, WIDE), lambda i: (0, jnp.minimum(i, chunks - 1)))
    return pl.pallas_call(
        functools.partial(down_kernel, blocks, slots, extra, chunks),
        grid=(chunks + 1,),
        in_specs=[pl.BlockSpec(hid.shape, lambda i: (0, 0)), w_out, w_out],
        out_specs=pl.BlockSpec((rows, WIDE), lambda i: (0, i)),
        out_shape=jax.ShapeDtypeStruct((rows, width + CHUNK), BF16),
        scratch_shapes=[pltpu.VMEM((rows, CHUNK), BF16), pltpu.VMEM((CHUNK // 128, rows, 128), F32)],
        compiler_params=pltpu.CompilerParams(vmem_limit_bytes=VMEM),
        cost_estimate=pl.CostEstimate(
            flops=4 * hid.shape[0] * width * half, bytes_accessed=2 * rows * width + 4 * width * half, transcendentals=0
        ),
    )(hid, wd0, wd1)


def after(value, *first):
    anywhere = pl.BlockSpec(memory_space=pl.ANY)
    return pl.pallas_call(
        lambda *refs: None,
        in_specs=[anywhere] * (1 + len(first)),
        out_specs=anywhere,
        out_shape=jax.ShapeDtypeStruct(value.shape, value.dtype),
        input_output_aliases={0: 0},
        cost_estimate=pl.CostEstimate(flops=0, bytes_accessed=0, transcendentals=0),
    )(value, *first)


def column(line):
    eye = iota((128, 128), 0) == iota((128, 128), 1)
    return jnp.concatenate(
        [
            jnp.sum(jnp.where(eye, line[:, at : at + 128], 0.0), axis=1, keepdims=True)
            for at in range(0, line.shape[1], 128)
        ],
        axis=0,
    )


def combine_kernel(experts, slots, extra, back, back_more, x, x_more, own, other, own_hid, other_hid, wg, wu, wd,
                   out, s_gate, s_up, s_down, wide, late):
    i = pl.program_id(0)
    more, parts = experts * extra, WIDE // CHUNK

    @pl.when(i == 0)
    def _():
        to_chunks(wide, x_more, late, experts, slots)

    total = jnp.dot(back[...], x[...], preferred_element_type=F32)
    for part in range(parts):
        lanes = slice(part * CHUNK, (part + 1) * CHUNK)
        at = pl.multiple_of((i * parts + part) * more, more)
        out[:, lanes] = (
            total[:, lanes] + jnp.dot(back_more[...], late[pl.ds(at, more), :], preferred_element_type=F32)
        ).astype(BF16)
    norm = column(jnp.sqrt(own[...] + other[...]))
    s_gate[...] = (jnp.abs(wg[...].astype(F32)) * norm).astype(BF16)
    s_up[...] = (jnp.abs(wu[...].astype(F32)) * norm).astype(BF16)
    half = wg.shape[1]
    norm = column(jnp.sqrt(own_hid[:, 0:half] + other_hid[:, half : 2 * half]))
    s_down[...] = (jnp.abs(wd[...].astype(F32)) * norm).astype(BF16)


def combine(back, back_more, returned, own, other, wg, wu, wd, experts, slots, extra):
    rows, wide = returned.shape
    width = wide - CHUNK
    chunks = width // WIDE
    count, half = back.shape[0], wg.shape[1]
    tall = pl.BlockSpec((WIDE, half), lambda i: (i, 0))
    flat = pl.BlockSpec((half, WIDE), lambda i: (0, i))
    sums = pl.BlockSpec((1, WIDE), lambda i: (0, i))
    last = pl.BlockSpec((1, WIDE), lambda i: (0, chunks))
    return pl.pallas_call(
        functools.partial(combine_kernel, experts, slots, extra),
        grid=(chunks,),
        in_specs=[
            pl.BlockSpec(back.shape, lambda i: (0, 0)),
            pl.BlockSpec(back_more.shape, lambda i: (0, 0)),
            pl.BlockSpec((rows, WIDE), lambda i: (0, i)),
            pl.BlockSpec((rows, CHUNK), lambda i: (0, width // CHUNK)),
            sums, sums, last, last,
            tall, tall, flat,
        ],
        out_specs=[pl.BlockSpec((count, WIDE), lambda i: (0, i)), tall, tall, flat],
        out_shape=[
            jax.ShapeDtypeStruct((count, width), BF16),
            jax.ShapeDtypeStruct(wg.shape, BF16),
            jax.ShapeDtypeStruct(wu.shape, BF16),
            jax.ShapeDtypeStruct(wd.shape, BF16),
        ],
        scratch_shapes=[pltpu.VMEM((CHUNK // 128, rows, 128), F32), pltpu.VMEM((rows, CHUNK), BF16)],
        compiler_params=pltpu.CompilerParams(vmem_limit_bytes=VMEM),
        cost_estimate=pl.CostEstimate(flops=4 * rows * count * width, bytes_accessed=6 * rows * wide, transcendentals=0),
    )(back, back_more, returned, returned, own, other, own, other, wg, wu, wd)


def swap(value):
    return lax.ppermute(value, "tp", [(0, 1), (1, 0)])


def exchange(value, experts, slots):
    value = value.reshape(experts, slots, value.shape[1])
    value = lax.all_to_all(value, "exp", split_axis=0, concat_axis=0, tiled=True)
    return value.reshape(experts * slots, value.shape[2])


def per_device(tokens, gate_weight, up_weight, down_weight, routes, gate_probs, valid_mask):
    count, top = routes.shape
    experts = lax.axis_size("exp")
    cap = max(2, count * top * 9 // (8 * experts))
    extra = 2
    slots = cap - extra
    w_gate, w_up, w_down = gate_weight[0], up_weight[0], down_weight[0]
    o_gate, o_up = swap(w_gate), swap(w_up)
    routes, valid_mask, gate_probs = routes.T, valid_mask.T, gate_probs.T
    sent, back, back_more = build(routes, valid_mask, gate_probs, tokens, experts, slots, extra)
    received = exchange(after(sent, o_gate, o_up), experts, slots)
    o_down = swap(copy_after(w_down, received))
    hid, sums = hidden_units(received, w_gate, o_gate, w_up, o_up, experts, slots, extra)
    other = swap(sums)
    outs = after(down(hid, w_down, o_down, experts, slots, extra), other)
    returned = exchange(outs, experts, slots)
    mixed, score_gate, score_up, score_down = combine(
        back, back_more, returned, sums, other, w_gate, w_up, w_down, experts, slots, extra
    )
    return (mixed, score_gate[None], score_up[None], score_down[None])


def solution(mesh):
    in_specs = (
        P(("exp", "tp"), None),
        P("exp", None, "tp"),
        P("exp", None, "tp"),
        P("exp", "tp", None),
        P(("exp", "tp"), None),
        P(("exp", "tp"), None),
        P(("exp", "tp"), None),
    )
    out_specs = (
        P(("exp", "tp"), None),
        P("exp", None, "tp"),
        P("exp", None, "tp"),
        P("exp", "tp", None),
    )
    return jax.shard_map(
        per_device, mesh=mesh, in_specs=in_specs, out_specs=out_specs, check_vma=False
    )
```

time: 311 us -> 305 us (0.981)
  Pallas kernels: 62.7 us -> 58.1 us
    pallas_call x2, Pallas kernels: 19 us -> 14.7 us  [the longest x1 11.8 us: combine(): pl.pallas_call(functools.partial(combine_kernel, experts, slots, extra),...]
where the time goes in v4:
time: 305 us; the launch traced here: 300 us
  blocking collectives  236 us (77%)
  Pallas kernels  58.1 us (19%)
    all_to_all x2, blocking collectives, exchange(): lax.all_to_all(value, 'exp', split_axis=0, concat_axis=0, tiled=True)  236 us
    pallas_call x1, Pallas kernels, hidden_units(): pl.pallas_call(functools.partial(hidden_kernel, blocks, slots, extra, chu...  22.2 us
    pallas_call x1, Pallas kernels, down(): pl.pallas_call(functools.partial(down_kernel, blocks, slots, extra, chunk...  12.6 us
    pallas_call x1, Pallas kernels, combine(): pl.pallas_call(functools.partial(combine_kernel, experts, slots, extra),...  11.8 us
    pallas_call x1, Pallas kernels, build(): pl.pallas_call(functools.partial(build_kernel, experts, slots, extra, chu...  8.62 us
  transfers between devices with their start and end apart: 4, of which 2 were waited for; matrix products, arithmetic and copies ran while one was open for 0% of the time, Pallas kernels for 14%

profile of v4, /device:TPU:50, one launch (start us, length us, event | category | flops | bytes accessed | tf_op | source)
XLA Modules:
  0.0 300.4 jit_solution(845616077588943300)
XLA Ops:
  0.6 0.1 collective-permute-start
  0.7 0.5 collective-permute-start.1
  1.2 8.6 %shard_map.102 = (bf16[1024,4736]{1,0:T(8,128)(2,1)}, bf16[128,1024]{1,0:T(8,128)(2,1)}, bf16[128,128]{1,0:T(8,128)(2,1)}) custom-call(s32[8,128]{1,0:T(8,128)} %bitcast.33, s32[8,128]{1,0:T(8,128)} %bitcast.34, f32[8,128]{1,0:T(8,128)} %bitcast.35, bf16[128,4096]{1,0:T(8,128)(2,1)} %tok.1), custom_call_target="tpu_custom_call" | custom-call | flops 2147483648 | bytes 8388608 | tf_op jit(solution)/shard_map/pallas_call | solution.py:102
  9.8 0.3 collective-permute-done.refs_1_.wg1
  10.1 0.0 copy-start
  10.1 1.1 collective-permute-done.1.refs_2_.wu1
  11.2 0.6 copy-done
  11.8 119.6 %all_to_all.10 = bf16[64,16,4736]{2,1,0:T(8,128)(2,1)} all-to-all(bf16[64,16,4736]{2,1,0:T(8,128)(2,1)} %bitcast.15), channel_id=1, replica_groups=mesh['exp'=64,'tp'=2] {'exp'}, dimensions={0} | all-to-all | bytes 19398656 | tf_op jit(solution)/shard_map/all_to_all | solution.py:389
  131.4 2.9 shard_map.105
  134.3 0.3 collective-permute-start.2
  134.5 22.2 %shard_map.104 = (bf16[1152,768]{1,0:T(8,128)(2,1)}, f32[1,5120]{1,0:T(1,128)}) custom-call(bf16[1024,4736]{1,0:T(8,128)(2,1)} %bitcast.17, bf16[1024,4736]{1,0:T(8,128)(2,1)} %bitcast.18, bf16[1024,4736]{1,0:T(8,128)(2,1)} %bitcast.19, bf16[4096,384]{1,0:T(8,128)(2,1)} %bitcast.25, bf16[4096,384]{1,0:T(8,128)(2,1)} %copy-done, bf16[4096,384]{1,0:T(8,128)(2,1)} %bitcast.28, ...), custom_call_target="tpu_custom_call" | custom-call | flops 14495514624 | bytes 20971520 | tf_op jit(solution)/shard_map/pallas_call | solution.py:232
  156.8 0.5 collective-permute-start.3
  157.2 0.0 collective-permute-done.2.wd1
  157.2 0.0 copy-start.2
  157.2 1.7 copy-done.2
  158.9 12.6 %shard_map.106.refs_0_ = bf16[1024,4608]{1,0:T(8,128)(2,1)} custom-call(bf16[1152,768]{1,0:T(8,128)(2,1)} %get-tuple-element.16.hid, bf16[384,4096]{1,0:T(8,128)(2,1)} %bitcast.22, bf16[384,4096]{1,0:T(8,128)(2,1)} %copy-done.2), custom_call_target="tpu_custom_call" | custom-call | flops 7247757312 | bytes 14680064 | tf_op jit(solution)/shard_map/pallas_call | solution.py:289
  171.5 0.0 collective-permute-done.3.refs_1_.other.other_hid
  171.5 0.0 copy-start.1
  171.5 0.6 copy-done.1
  172.1 116.3 %all_to_all.11 = bf16[64,16,4608]{2,1,0:T(8,128)(2,1)} all-to-all(bf16[64,16,4608]{2,1,0:T(8,128)(2,1)} %bitcast.20), channel_id=1, replica_groups=mesh['exp'=64,'tp'=2] {'exp'}, dimensions={0} | all-to-all | bytes 18874368 | tf_op jit(solution)/shard_map/all_to_all | solution.py:389
  288.4 11.8 %shard_map.108 = (bf16[128,4096]{1,0:T(8,128)(2,1)}, bf16[4096,384]{1,0:T(8,128)(2,1)}, bf16[4096,384]{1,0:T(8,128)(2,1)}, bf16[384,4096]{1,0:T(8,128)(2,1)}) custom-call(bf16[128,1024]{1,0:T(8,128)(2,1)} %get-tuple-element.13.back, bf16[128,128]{1,0:T(8,128)(2,1)} %get-tuple-element.14.back_more, bf16[1024,4608]{1,0:T(8,128)(2,1)} %bitcast.13, ...), custom_call_target="tpu_custom_call" | custom-call | flops 2147483648 | bytes 28311552 | tf_op jit(solution)/shard_map/pallas_call | solution.py:359
  (2 shorter events, 0.0 us)
Async XLA Ops:
  0.6 9.5 %collective-permute-start = (bf16[4096,384]{1,0:T(8,128)(2,1)}, bf16[4096,384]{1,0:T(8,128)(2,1)S(1)}, u32[]{:S(2)}, u32[]{:S(2)}) collective-permute-start(bf16[4096,384]{1,0:T(8,128)(2,1)} %bitcast.24), channel_id=1, source_target_pairs={{0,1},{1,0},{2,3},{3,2},{4,5},{5,4},{6,7},{7,6},{8,9},{9,8},{10,11... | collective-permute-start | bytes 9437192 | tf_op jit(solution)/shard_map/ppermute | solution.py:384
  0.7 10.5 %collective-permute-start.1 = (bf16[4096,384]{1,0:T(8,128)(2,1)}, bf16[4096,384]{1,0:T(8,128)(2,1)}, u32[]{:S(2)}, u32[]{:S(2)}) collective-permute-start(bf16[4096,384]{1,0:T(8,128)(2,1)} %bitcast.27), channel_id=1, source_target_pairs={{0,1},{1,0},{2,3},{3,2},{4,5},{5,4},{6,7},{7,6},{8,9},{9,8},{10,11... | collective-permute-start | bytes 9437192 | tf_op jit(solution)/shard_map/ppermute | solution.py:384
  10.1 1.7 copy-start
  134.3 23.0 %collective-permute-start.2 = (bf16[384,4096]{1,0:T(8,128)(2,1)}, bf16[384,4096]{1,0:T(8,128)(2,1)S(1)}, u32[]{:S(2)}, u32[]{:S(2)}) collective-permute-start(bf16[384,4096]{1,0:T(8,128)(2,1)} %shard_map.105), channel_id=1, source_target_pairs={{0,1},{1,0},{2,3},{3,2},{4,5},{5,4},{6,7},{7,6},{8,9},{9,8},{10,11... | collective-permute-start | bytes 9437192 | tf_op jit(solution)/shard_map/ppermute | solution.py:384
  156.8 14.8 %collective-permute-start.3 = (f32[1,5120]{1,0:T(1,128)}, f32[1,5120]{1,0:T(1,128)S(1)}, u32[]{:S(2)}, u32[]{:S(2)}) collective-permute-start(f32[1,5120]{1,0:T(1,128)} %get-tuple-element.17.own.own_hid), channel_id=1, source_target_pairs={{0,1},{1,0},{2,3},{3,2},{4,5},{5,4},{6,7},{7,6},{8,9},{9,8},{10,11... | collective-permute-start | bytes 61448 | tf_op jit(solution)/shard_map/ppermute | solution.py:384
  157.2 1.7 copy-start.2
  171.5 0.6 copy-start.1

commit v5 on v4

--- a/solution.py
+++ b/solution.py
@@ -10,7 +10,9 @@
 BF16, F32 = jnp.bfloat16, jnp.float32
 CHUNK = 512
 WIDE = 1024
-PIECES = 3
+PIECES = 8
+DOWN_PIECES = 2
+NARROW = 1024
 VMEM = 56 * 1024 * 1024
 
 
@@ -55,7 +57,7 @@
     return jnp.where(named > 0, place, -1.0).astype(jnp.int32), weight
 
 
-def build_kernel(experts, slots, extra, chunks, routes, valid, probs, tok, out, back, back_more, sel_scr, pick_scr, stack, wide, w_scr):
+def build_kernel(experts, slots, extra, chunks, routes, valid, probs, tok, wd, out, back, back_more, wd_copy, sel_scr, pick_scr, stack, wide, w_scr):
     i = pl.program_id(0)
     more = experts * extra
     count = routes.shape[1]
@@ -82,6 +84,7 @@
 
     @pl.when(i < chunks)
     def _():
+        wd_copy[...] = wd[...]
         out[...] = jnp.dot(sel_scr[...], tok[...], preferred_element_type=F32).astype(BF16)
         late = jnp.dot(pick_scr[...], tok[...], preferred_element_type=F32).astype(BF16)
         for part in range(WIDE // CHUNK):
@@ -94,24 +97,27 @@
         out[:, CHUNK : CHUNK + 128] = w_scr[...]
 
 
-def build(routes, valid, probs, tokens, experts, slots, extra):
+def build(routes, valid, probs, tokens, wd, experts, slots, extra):
     count, width = tokens.shape
     chunks = width // WIDE
     rows = experts * slots
     small = pl.BlockSpec((routes.shape[0], count), lambda i: (0, 0))
+    flat = pl.BlockSpec((wd.shape[0], WIDE), lambda i: (0, jnp.minimum(i, chunks - 1)))
     return pl.pallas_call(
         functools.partial(build_kernel, experts, slots, extra, chunks),
         grid=(chunks + 1,),
-        in_specs=[small, small, small, pl.BlockSpec((count, WIDE), lambda i: (0, jnp.minimum(i, chunks - 1)))],
+        in_specs=[small, small, small, pl.BlockSpec((count, WIDE), lambda i: (0, jnp.minimum(i, chunks - 1))), flat],
         out_specs=[
             pl.BlockSpec((rows, WIDE), lambda i: (0, i)),
             pl.BlockSpec((count, rows), lambda i: (0, 0)),
             pl.BlockSpec((count, experts * extra), lambda i: (0, 0)),
+            flat,
         ],
         out_shape=[
             jax.ShapeDtypeStruct((rows, width + CHUNK + 128), BF16),
             jax.ShapeDtypeStruct((count, rows), BF16),
             jax.ShapeDtypeStruct((count, experts * extra), BF16),
+            jax.ShapeDtypeStruct(wd.shape, BF16),
         ],
         scratch_shapes=[
             pltpu.VMEM((rows, count), BF16),
@@ -122,40 +128,7 @@
         ],
         compiler_params=pltpu.CompilerParams(vmem_limit_bytes=VMEM),
         cost_estimate=pl.CostEstimate(flops=4 * rows * count * width, bytes_accessed=2 * rows * width, transcendentals=0),
-    )(routes, valid, probs, tokens)
-
-
-def copy_kernel(given, first, copied, held, sem_in, sem_out):
-    count = held.shape[0]
-    pieces = [pl.ds(at * WIDE, WIDE) for at in range(count)]
-    ins = [pltpu.make_async_copy(given.at[:, p], held.at[at], sem_in.at[at]) for at, p in enumerate(pieces)]
-    outs = [pltpu.make_async_copy(held.at[at], copied.at[:, p], sem_out.at[at]) for at, p in enumerate(pieces)]
-    for copy in ins:
-        copy.start()
-    for at in range(count):
-        ins[at].wait()
-        outs[at].start()
-    for copy in outs:
-        copy.wait()
-
-
-def copy_after(value, first):
-    high, width = value.shape
-    count = width // WIDE
-    anywhere = pl.BlockSpec(memory_space=pl.ANY)
-    return pl.pallas_call(
-        copy_kernel,
-        in_specs=[anywhere, anywhere],
-        out_specs=anywhere,
-        out_shape=jax.ShapeDtypeStruct(value.shape, value.dtype),
-        scratch_shapes=[
-            pltpu.VMEM((count, high, WIDE), value.dtype),
-            pltpu.SemaphoreType.DMA((count,)),
-            pltpu.SemaphoreType.DMA((count,)),
-        ],
-        compiler_params=pltpu.CompilerParams(vmem_limit_bytes=VMEM),
-        cost_estimate=pl.CostEstimate(flops=0, bytes_accessed=4 * high * width, transcendentals=0),
-    )(value, first)
+    )(routes, valid, probs, tokens, wd)
 
 
 def hidden_kernel(blocks, slots, extra, chunks, x, x_more, x_w, wg0, wg1, wu0, wu1, hid, sq, xs, acc0, acc1, w_col,
@@ -171,17 +144,33 @@
             at = pl.multiple_of((i * parts + part) * more, more)
             xs[rows : rows + more, part * CHUNK : (part + 1) * CHUNK] = late[pl.ds(at, more), :]
 
-    def squares():
-        for lane in range(0, WIDE, 128):
-            part = xs[:, lane : lane + 128].astype(F32)
-            sq[:, lane : lane + 128] = jnp.sum(part * part * w_col[...], axis=0, keepdims=True)
-
-    def products(at, high):
-        piece = xs[at : at + high, :]
-        return (
-            jnp.dot(piece, jnp.concatenate([wg0[...], wu0[...]], axis=1), preferred_element_type=F32),
-            jnp.dot(piece, jnp.concatenate([wg1[...], wu1[...]], axis=1), preferred_element_type=F32),
-        )
+    def squares(lane):
+        part = xs[:, lane : lane + 128].astype(F32)
+        sq[:, lane : lane + 128] = jnp.sum(part * part * w_col[...], axis=0, keepdims=True)
+
+    def products(use):
+        high = (rows + more) // PIECES
+        share = WIDE // PIECES
+        for piece in range(PIECES):
+            span = slice(piece * high, (piece + 1) * high)
+            value = xs[span, :]
+            for start, acc, gate, up in ((0, acc0, wg0, wu0), (half, acc1, wg1, wu1)):
+                use(span, start, acc, jnp.dot(
+                    value, jnp.concatenate([gate[...], up[...]], axis=1), preferred_element_type=F32
+                ))
+            for lane in range(piece * share, (piece + 1) * share, 128):
+                squares(lane)
+
+    def put(span, start, acc, product):
+        acc[span, :] = product
+
+    def add(span, start, acc, product):
+        acc[span, :] += product
+
+    def finish(span, start, acc, product):
+        gate = acc[span, 0:half] + product[:, 0:half]
+        up = acc[span, half : 2 * half] + product[:, half : 2 * half]
+        hid[span, start : start + half] = (gate * (0.5 + 0.5 * jnp.tanh(0.5 * gate)) * up).astype(BF16)
 
     @pl.when(i == 0)
     def _():
@@ -192,28 +181,17 @@
             w_col[rows + r * blocks : rows + (r + 1) * blocks, :] = jnp.broadcast_to(w_more[:, 1:2], (blocks, 128))
         to_chunks(wide, x_more, late, blocks, slots)
         fill()
-        acc0[...], acc1[...] = products(0, rows + more)
-        squares()
+        products(put)
 
     @pl.when((i > 0) & (i < chunks - 1))
     def _():
         fill()
-        first, second = products(0, rows + more)
-        acc0[...] += first
-        acc1[...] += second
-        squares()
+        products(add)
 
     @pl.when(i == chunks - 1)
     def _():
         fill()
-        squares()
-        high = (rows + more) // PIECES
-        for at in range(0, rows + more, high):
-            span = slice(at, at + high)
-            for start, acc, product in zip((0, half), (acc0, acc1), products(at, high)):
-                gate = acc[span, 0:half] + product[:, 0:half]
-                up = acc[span, half : 2 * half] + product[:, half : 2 * half]
-                hid[span, start : start + half] = (gate * (0.5 + 0.5 * jnp.tanh(0.5 * gate)) * up).astype(BF16)
+        products(finish)
 
     @pl.when(i == chunks)
     def _():
@@ -268,13 +246,16 @@
 
     @pl.when(i < chunks)
     def _():
-        result = jnp.dot(
-            hid[...], jnp.concatenate([wd0[...], wd1[...]], axis=0), preferred_element_type=F32
-        ).astype(BF16)
-        out[...] = result[0:rows]
+        both = jnp.concatenate([wd0[...], wd1[...]], axis=0)
+        high = rows // DOWN_PIECES
+        for at in range(0, rows, high):
+            out[at : at + high, :] = jnp.dot(
+                hid[at : at + high, :], both, preferred_element_type=F32
+            ).astype(BF16)
+        result = jnp.dot(hid[rows : rows + more, :], both, preferred_element_type=F32).astype(BF16)
         for part in range(parts):
             at = pl.multiple_of((i * parts + part) * more, more)
-            stack[pl.ds(at, more), :] = result[rows : rows + more, part * CHUNK : (part + 1) * CHUNK]
+            stack[pl.ds(at, more), :] = result[:, part * CHUNK : (part + 1) * CHUNK]
 
     @pl.when(i == chunks)
     def _():
@@ -326,7 +307,7 @@
 def combine_kernel(experts, slots, extra, back, back_more, x, x_more, own, other, own_hid, other_hid, wg, wu, wd,
                    out, s_gate, s_up, s_down, wide, late):
     i = pl.program_id(0)
-    more, parts = experts * extra, WIDE // CHUNK
+    more, parts = experts * extra, NARROW // CHUNK
 
     @pl.when(i == 0)
     def _():
@@ -350,24 +331,24 @@
 def combine(back, back_more, returned, own, other, wg, wu, wd, experts, slots, extra):
     rows, wide = returned.shape
     width = wide - CHUNK
-    chunks = width // WIDE
+    chunks = width // NARROW
     count, half = back.shape[0], wg.shape[1]
-    tall = pl.BlockSpec((WIDE, half), lambda i: (i, 0))
-    flat = pl.BlockSpec((half, WIDE), lambda i: (0, i))
-    sums = pl.BlockSpec((1, WIDE), lambda i: (0, i))
-    last = pl.BlockSpec((1, WIDE), lambda i: (0, chunks))
+    tall = pl.BlockSpec((NARROW, half), lambda i: (i, 0))
+    flat = pl.BlockSpec((half, NARROW), lambda i: (0, i))
+    sums = pl.BlockSpec((1, NARROW), lambda i: (0, i))
+    last = pl.BlockSpec((1, WIDE), lambda i: (0, width // WIDE))
     return pl.pallas_call(
         functools.partial(combine_kernel, experts, slots, extra),
         grid=(chunks,),
         in_specs=[
             pl.BlockSpec(back.shape, lambda i: (0, 0)),
             pl.BlockSpec(back_more.shape, lambda i: (0, 0)),
-            pl.BlockSpec((rows, WIDE), lambda i: (0, i)),
+            pl.BlockSpec((rows, NARROW), lambda i: (0, i)),
             pl.BlockSpec((rows, CHUNK), lambda i: (0, width // CHUNK)),
             sums, sums, last, last,
             tall, tall, flat,
         ],
-        out_specs=[pl.BlockSpec((count, WIDE), lambda i: (0, i)), tall, tall, flat],
+        out_specs=[pl.BlockSpec((count, NARROW), lambda i: (0, i)), tall, tall, flat],
         out_shape=[
             jax.ShapeDtypeStruct((count, width), BF16),
             jax.ShapeDtypeStruct(wg.shape, BF16),
@@ -399,9 +380,11 @@
     w_gate, w_up, w_down = gate_weight[0], up_weight[0], down_weight[0]
     o_gate, o_up = swap(w_gate), swap(w_up)
     routes, valid_mask, gate_probs = routes.T, valid_mask.T, gate_probs.T
-    sent, back, back_more = build(routes, valid_mask, gate_probs, tokens, experts, slots, extra)
+    sent, back, back_more, late_down = build(
+        routes, valid_mask, gate_probs, tokens, w_down, experts, slots, extra
+    )
     received = exchange(after(sent, o_gate, o_up), experts, slots)
-    o_down = swap(copy_after(w_down, received))
+    o_down = swap(after(late_down, received))
     hid, sums = hidden_units(received, w_gate, o_gate, w_up, o_up, experts, slots, extra)
     other = swap(sums)
     outs = after(down(hid, w_down, o_down, experts, slots, extra), other)

time: 305 us -> 303 us (level)
  transfers between devices with their start and end apart: 4 -> 4, of which waited for: 2 -> 0; matrix products, arithmetic and copies ran while one was open for 0% -> 0% of each run, Pallas kernels for 14% -> 15%
where the time goes in v5:
time: 303 us; the launch traced here: 298 us
  blocking collectives  236 us (78%)
  Pallas kernels  56.4 us (19%)
  local copies, waits for them, and re-layouts  3.91 us (1%)
    all_to_all x2, blocking collectives, exchange(): lax.all_to_all(value, 'exp', split_axis=0, concat_axis=0, tiled=True)  236 us
    pallas_call x1, Pallas kernels, hidden_units(): pl.pallas_call(functools.partial(hidden_kernel, blocks, slots, extra, chu...  22 us
    pallas_call x1, Pallas kernels, down(): pl.pallas_call(functools.partial(down_kernel, blocks, slots, extra, chunk...  12.6 us
    pallas_call x1, Pallas kernels, combine(): pl.pallas_call(functools.partial(combine_kernel, experts, slots, extra),...  11.8 us
    pallas_call x1, Pallas kernels, build(): pl.pallas_call(functools.partial(build_kernel, experts, slots, extra, chu...  10 us
  transfers between devices with their start and end apart: 4, of which 0 were waited for; matrix products, arithmetic and copies ran while one was open for 0% of the time, Pallas kernels for 15%

profile of v5, /device:TPU:50, one launch (start us, length us, event | category | flops | bytes accessed | tf_op | source)
XLA Modules:
  0.0 298.1 jit_solution(5807279603284542061)
XLA Ops:
  0.6 0.1 collective-permute-start
  0.7 0.5 collective-permute-start.1
  1.2 10.0 %shard_map.102 = (bf16[1024,4736]{1,0:T(8,128)(2,1)}, bf16[128,1024]{1,0:T(8,128)(2,1)}, bf16[128,128]{1,0:T(8,128)(2,1)}, bf16[384,4096]{1,0:T(8,128)(2,1)}) custom-call(s32[8,128]{1,0:T(8,128)} %bitcast.33, s32[8,128]{1,0:T(8,128)} %bitcast.34, f32[8,128]{1,0:T(8,128)} %bitcast.35, bf16[128,4096]{1,0:T(8,128)(2,1)} %tok.1, bf16[384,4096]{1,0:T(8,128)(2,1)} %bitcast.21), custom_call_target="tpu_custom_call" | custom-call | flops 2147483648 | bytes 8388608 | tf_op jit(solution)/shard_map/pallas_call | solution.py:106
  11.2 0.0 collective-permute-done.refs_1_.wg1
  11.2 0.0 copy-start
  11.3 0.0 collective-permute-done.1.refs_2_.wu1
  11.3 1.6 copy-done
  12.9 119.6 %all_to_all.10 = bf16[64,16,4736]{2,1,0:T(8,128)(2,1)} all-to-all(bf16[64,16,4736]{2,1,0:T(8,128)(2,1)} %bitcast.15), channel_id=1, replica_groups=mesh['exp'=64,'tp'=2] {'exp'}, dimensions={0} | all-to-all | bytes 19398656 | tf_op jit(solution)/shard_map/all_to_all | solution.py:370
  132.5 0.0 collective-permute-start.2
  132.5 22.0 %shard_map.104 = (bf16[1152,768]{1,0:T(8,128)(2,1)}, f32[1,5120]{1,0:T(1,128)}) custom-call(bf16[1024,4736]{1,0:T(8,128)(2,1)} %bitcast.17, bf16[1024,4736]{1,0:T(8,128)(2,1)} %bitcast.18, bf16[1024,4736]{1,0:T(8,128)(2,1)} %bitcast.19, bf16[4096,384]{1,0:T(8,128)(2,1)} %bitcast.25, bf16[4096,384]{1,0:T(8,128)(2,1)} %copy-done, bf16[4096,384]{1,0:T(8,128)(2,1)} %bitcast.28, ...), custom_call_target="tpu_custom_call" | custom-call | flops 14495514624 | bytes 20971520 | tf_op jit(solution)/shard_map/pallas_call | solution.py:210
  154.5 0.4 collective-permute-start.3
  154.9 0.0 collective-permute-done.2.wd1
  154.9 0.0 copy-start.2
  154.9 1.7 copy-done.2
  156.6 12.6 %shard_map.106.refs_0_ = bf16[1024,4608]{1,0:T(8,128)(2,1)} custom-call(bf16[1152,768]{1,0:T(8,128)(2,1)} %get-tuple-element.17.hid, bf16[384,4096]{1,0:T(8,128)(2,1)} %bitcast.22, bf16[384,4096]{1,0:T(8,128)(2,1)} %copy-done.2), custom_call_target="tpu_custom_call" | custom-call | flops 7247757312 | bytes 14680064 | tf_op jit(solution)/shard_map/pallas_call | solution.py:270
  169.2 0.0 collective-permute-done.3.refs_1_.other.other_hid
  169.2 0.0 copy-start.1
  169.2 0.6 copy-done.1
  169.8 116.3 %all_to_all.11 = bf16[64,16,4608]{2,1,0:T(8,128)(2,1)} all-to-all(bf16[64,16,4608]{2,1,0:T(8,128)(2,1)} %bitcast.20), channel_id=1, replica_groups=mesh['exp'=64,'tp'=2] {'exp'}, dimensions={0} | all-to-all | bytes 18874368 | tf_op jit(solution)/shard_map/all_to_all | solution.py:370
  286.1 11.8 %shard_map.108 = (bf16[128,4096]{1,0:T(8,128)(2,1)}, bf16[4096,384]{1,0:T(8,128)(2,1)}, bf16[4096,384]{1,0:T(8,128)(2,1)}, bf16[384,4096]{1,0:T(8,128)(2,1)}) custom-call(bf16[128,1024]{1,0:T(8,128)(2,1)} %get-tuple-element.14.back, bf16[128,128]{1,0:T(8,128)(2,1)} %get-tuple-element.15.back_more, bf16[1024,4608]{1,0:T(8,128)(2,1)} %bitcast.13, ...), custom_call_target="tpu_custom_call" | custom-call | flops 2147483648 | bytes 28311552 | tf_op jit(solution)/shard_map/pallas_call | solution.py:340
  (3 shorter events, 0.0 us)
Async XLA Ops:
  0.6 10.6 %collective-permute-start = (bf16[4096,384]{1,0:T(8,128)(2,1)}, bf16[4096,384]{1,0:T(8,128)(2,1)S(1)}, u32[]{:S(2)}, u32[]{:S(2)}) collective-permute-start(bf16[4096,384]{1,0:T(8,128)(2,1)} %bitcast.24), channel_id=1, source_target_pairs={{0,1},{1,0},{2,3},{3,2},{4,5},{5,4},{6,7},{7,6},{8,9},{9,8},{10,11... | collective-permute-start | bytes 9437192 | tf_op jit(solution)/shard_map/ppermute | solution.py:365
  0.7 10.5 %collective-permute-start.1 = (bf16[4096,384]{1,0:T(8,128)(2,1)}, bf16[4096,384]{1,0:T(8,128)(2,1)}, u32[]{:S(2)}, u32[]{:S(2)}) collective-permute-start(bf16[4096,384]{1,0:T(8,128)(2,1)} %bitcast.27), channel_id=1, source_target_pairs={{0,1},{1,0},{2,3},{3,2},{4,5},{5,4},{6,7},{7,6},{8,9},{9,8},{10,11... | collective-permute-start | bytes 9437192 | tf_op jit(solution)/shard_map/ppermute | solution.py:365
  11.2 1.7 copy-start
  132.5 22.4 %collective-permute-start.2 = (bf16[384,4096]{1,0:T(8,128)(2,1)}, bf16[384,4096]{1,0:T(8,128)(2,1)S(1)}, u32[]{:S(2)}, u32[]{:S(2)}) collective-permute-start(bf16[384,4096]{1,0:T(8,128)(2,1)} %shard_map.105), channel_id=1, source_target_pairs={{0,1},{1,0},{2,3},{3,2},{4,5},{5,4},{6,7},{7,6},{8,9},{9,8},{10,11... | collective-permute-start | bytes 9437192 | tf_op jit(solution)/shard_map/ppermute | solution.py:365
  154.5 14.7 %collective-permute-start.3 = (f32[1,5120]{1,0:T(1,128)}, f32[1,5120]{1,0:T(1,128)S(1)}, u32[]{:S(2)}, u32[]{:S(2)}) collective-permute-start(f32[1,5120]{1,0:T(1,128)} %get-tuple-element.19.own.own_hid), channel_id=1, source_target_pairs={{0,1},{1,0},{2,3},{3,2},{4,5},{5,4},{6,7},{7,6},{8,9},{9,8},{10,11... | collective-permute-start | bytes 61448 | tf_op jit(solution)/shard_map/ppermute | solution.py:365
  154.9 1.7 copy-start.2
  169.2 0.6 copy-start.1

commit v6 on v5

--- a/solution.py
+++ b/solution.py
@@ -14,6 +14,7 @@
 DOWN_PIECES = 2
 NARROW = 1024
 VMEM = 56 * 1024 * 1024
+COMBINE_VMEM = 28 * 1024 * 1024
 
 
 def iota(shape, dim):
@@ -356,7 +357,7 @@
             jax.ShapeDtypeStruct(wd.shape, BF16),
         ],
         scratch_shapes=[pltpu.VMEM((CHUNK // 128, rows, 128), F32), pltpu.VMEM((rows, CHUNK), BF16)],
-        compiler_params=pltpu.CompilerParams(vmem_limit_bytes=VMEM),
+        compiler_params=pltpu.CompilerParams(vmem_limit_bytes=COMBINE_VMEM),
         cost_estimate=pl.CostEstimate(flops=4 * rows * count * width, bytes_accessed=6 * rows * wide, transcendentals=0),
     )(back, back_more, returned, returned, own, other, own, other, wg, wu, wd)
 

time: 303 us -> 299 us (0.987)
  Pallas kernels: 56.4 us -> 51.9 us
    pallas_call x1, Pallas kernels: 11.8 us -> 7.36 us  [combine(): pl.pallas_call(functools.partial(combine_kernel, experts, slots, extra),...]
where the time goes in v6:
time: 299 us; the launch traced here: 294 us
  blocking collectives  236 us (79%)
  Pallas kernels  51.9 us (17%)
  local copies, waits for them, and re-layouts  3.95 us (1%)
    all_to_all x2, blocking collectives, exchange(): lax.all_to_all(value, 'exp', split_axis=0, concat_axis=0, tiled=True)  236 us
    pallas_call x1, Pallas kernels, hidden_units(): pl.pallas_call(functools.partial(hidden_kernel, blocks, slots, extra, chu...  22 us
    pallas_call x1, Pallas kernels, down(): pl.pallas_call(functools.partial(down_kernel, blocks, slots, extra, chunk...  12.5 us
    pallas_call x1, Pallas kernels, build(): pl.pallas_call(functools.partial(build_kernel, experts, slots, extra, chu...  10 us
    pallas_call x1, Pallas kernels, combine(): pl.pallas_call(functools.partial(combine_kernel, experts, slots, extra),...  7.36 us
  transfers between devices with their start and end apart: 4, of which 0 were waited for; matrix products, arithmetic and copies ran while one was open for 0% of the time, Pallas kernels for 15%

profile of v6, /device:TPU:50, one launch (start us, length us, event | category | flops | bytes accessed | tf_op | source)
XLA Modules:
  0.0 293.6 jit_solution(977624070660770230)
XLA Ops:
  0.6 0.1 collective-permute-start
  0.7 0.5 collective-permute-start.1
  1.2 10.0 %shard_map.102 = (bf16[1024,4736]{1,0:T(8,128)(2,1)}, bf16[128,1024]{1,0:T(8,128)(2,1)}, bf16[128,128]{1,0:T(8,128)(2,1)}, bf16[384,4096]{1,0:T(8,128)(2,1)}) custom-call(s32[8,128]{1,0:T(8,128)} %bitcast.33, s32[8,128]{1,0:T(8,128)} %bitcast.34, f32[8,128]{1,0:T(8,128)} %bitcast.35, bf16[128,4096]{1,0:T(8,128)(2,1)} %tok.1, bf16[384,4096]{1,0:T(8,128)(2,1)} %bitcast.15), custom_call_target="tpu_custom_call" | custom-call | flops 2147483648 | bytes 8388608 | tf_op jit(solution)/shard_map/pallas_call | solution.py:107
  11.2 0.0 collective-permute-done.refs_1_.wg1
  11.2 0.0 copy-start.8
  11.3 0.0 collective-permute-done.1.refs_2_.wu1
  11.3 1.6 copy-done.8
  12.9 119.6 %all_to_all.10 = bf16[64,16,4736]{2,1,0:T(8,128)(2,1)} all-to-all(bf16[64,16,4736]{2,1,0:T(8,128)(2,1)} %bitcast.24), channel_id=1, replica_groups=mesh['exp'=64,'tp'=2] {'exp'}, dimensions={0} | all-to-all | bytes 19398656 | tf_op jit(solution)/shard_map/all_to_all | solution.py:371
  132.5 0.0 collective-permute-start.2
  132.5 22.0 %shard_map.104 = (bf16[1152,768]{1,0:T(8,128)(2,1)}, f32[1,5120]{1,0:T(1,128)}) custom-call(bf16[1024,4736]{1,0:T(8,128)(2,1)} %bitcast.26, bf16[1024,4736]{1,0:T(8,128)(2,1)} %bitcast.27, bf16[1024,4736]{1,0:T(8,128)(2,1)} %bitcast.28, bf16[4096,384]{1,0:T(8,128)(2,1)} %bitcast.19, bf16[4096,384]{1,0:T(8,128)(2,1)} %copy-done.8, ...), custom_call_target="tpu_custom_call" | custom-call | flops 14495514624 | bytes 20971520 | tf_op jit(solution)/shard_map/pallas_call | solution.py:211
  154.5 0.4 collective-permute-start.3
  154.9 0.0 collective-permute-done.2.wd1
  154.9 0.0 copy-start.9
  154.9 1.7 copy-done.9
  156.6 12.5 %shard_map.106.refs_0_ = bf16[1024,4608]{1,0:T(8,128)(2,1)} custom-call(bf16[1152,768]{1,0:T(8,128)(2,1)} %get-tuple-element.17.hid, bf16[384,4096]{1,0:T(8,128)(2,1)} %bitcast.16, bf16[384,4096]{1,0:T(8,128)(2,1)} %copy-done.9), custom_call_target="tpu_custom_call" | custom-call | flops 7247757312 | bytes 14680064 | tf_op jit(solution)/shard_map/pallas_call | solution.py:271
  169.1 0.0 collective-permute-done.3.refs_1_.other.other_hid
  169.1 0.0 copy-start.4
  169.1 0.6 copy-done.4
  169.7 0.0 copy-start
  169.7 0.0 copy-start.1
  169.7 0.0 copy-start.2
  169.7 0.0 copy-start.3
  169.7 0.0 copy-start.5
  169.7 0.0 copy-start.6
  169.7 0.0 copy-start.7
  169.8 116.5 %all_to_all.11 = bf16[64,16,4608]{2,1,0:T(8,128)(2,1)S(1)} all-to-all(bf16[64,16,4608]{2,1,0:T(8,128)(2,1)} %bitcast.29), channel_id=1, replica_groups=mesh['exp'=64,'tp'=2] {'exp'}, dimensions={0} | all-to-all | bytes 18874368 | tf_op jit(solution)/shard_map/all_to_all | solution.py:371
  286.2 0.0 copy-done
  286.2 0.0 copy-done.1
  286.2 0.0 copy-done.2
  286.2 0.0 copy-done.3
  286.2 0.0 copy-done.5
  286.2 0.0 copy-done.6
  286.3 0.0 copy-done.7
  286.3 7.4 %shard_map.108 = (bf16[128,4096]{1,0:T(8,128)(2,1)}, bf16[4096,384]{1,0:T(8,128)(2,1)}, bf16[4096,384]{1,0:T(8,128)(2,1)}, bf16[384,4096]{1,0:T(8,128)(2,1)}) custom-call(bf16[128,1024]{1,0:T(8,128)(2,1)S(1)} %copy-done.3, bf16[128,128]{1,0:T(8,128)(2,1)S(1)} %copy-done.7, bf16[1024,4608]{1,0:T(8,128)(2,1)S(1)} %bitcast.13, bf16[1024,4608]{1,0:T(8,128)(2,1)S(1)} %bitcast.14, ...), custom_call_target="tpu_custom_call" | custom-call | flops 2147483648 | bytes 28311552 | tf_op jit(solution)/shard_map/pallas_call | solution.py:341
  (3 shorter events, 0.0 us)
Async XLA Ops:
  0.6 10.6 %collective-permute-start = (bf16[4096,384]{1,0:T(8,128)(2,1)}, bf16[4096,384]{1,0:T(8,128)(2,1)S(1)}, u32[]{:S(2)}, u32[]{:S(2)}) collective-permute-start(bf16[4096,384]{1,0:T(8,128)(2,1)} %bitcast.18), channel_id=1, source_target_pairs={{0,1},{1,0},{2,3},{3,2},{4,5},{5,4},{6,7},{7,6},{8,9},{9,8},{10,11... | collective-permute-start | bytes 9437192 | tf_op jit(solution)/shard_map/ppermute | solution.py:366
  0.7 10.5 %collective-permute-start.1 = (bf16[4096,384]{1,0:T(8,128)(2,1)}, bf16[4096,384]{1,0:T(8,128)(2,1)}, u32[]{:S(2)}, u32[]{:S(2)}) collective-permute-start(bf16[4096,384]{1,0:T(8,128)(2,1)} %bitcast.21), channel_id=1, source_target_pairs={{0,1},{1,0},{2,3},{3,2},{4,5},{5,4},{6,7},{7,6},{8,9},{9,8},{10,11... | collective-permute-start | bytes 9437192 | tf_op jit(solution)/shard_map/ppermute | solution.py:366
  11.2 1.7 copy-start.8
  132.5 22.4 %collective-permute-start.2 = (bf16[384,4096]{1,0:T(8,128)(2,1)}, bf16[384,4096]{1,0:T(8,128)(2,1)S(1)}, u32[]{:S(2)}, u32[]{:S(2)}) collective-permute-start(bf16[384,4096]{1,0:T(8,128)(2,1)} %shard_map.105), channel_id=1, source_target_pairs={{0,1},{1,0},{2,3},{3,2},{4,5},{5,4},{6,7},{7,6},{8,9},{9,8},{10,11... | collective-permute-start | bytes 9437192 | tf_op jit(solution)/shard_map/ppermute | solution.py:366
  154.5 14.6 %collective-permute-start.3 = (f32[1,5120]{1,0:T(1,128)}, f32[1,5120]{1,0:T(1,128)S(1)}, u32[]{:S(2)}, u32[]{:S(2)}) collective-permute-start(f32[1,5120]{1,0:T(1,128)} %get-tuple-element.19.own.own_hid), channel_id=1, source_target_pairs={{0,1},{1,0},{2,3},{3,2},{4,5},{5,4},{6,7},{7,6},{8,9},{9,8},{10,11... | collective-permute-start | bytes 61448 | tf_op jit(solution)/shard_map/ppermute | solution.py:366
  154.9 1.7 copy-start.9
  169.1 0.6 copy-start.4
  169.7 116.5 %copy-start = (bf16[1,384,4096]{2,1,0:T(8,128)(2,1)S(1)}, bf16[1,384,4096]{2,1,0:T(8,128)(2,1)}, u32[]{:S(2)}) copy-start(bf16[1,384,4096]{2,1,0:T(8,128)(2,1)} %param.10) | copy-start | bytes 9437188
  169.7 116.5 %copy-start.1 = (bf16[1,4096,384]{2,1,0:T(8,128)(2,1)S(1)}, bf16[1,4096,384]{2,1,0:T(8,128)(2,1)}, u32[]{:S(2)}) copy-start(bf16[1,4096,384]{2,1,0:T(8,128)(2,1)} %param.8) | copy-start | bytes 9437188
  169.7 116.5 %copy-start.2 = (bf16[1,4096,384]{2,1,0:T(8,128)(2,1)S(1)}, bf16[1,4096,384]{2,1,0:T(8,128)(2,1)}, u32[]{:S(2)}) copy-start(bf16[1,4096,384]{2,1,0:T(8,128)(2,1)} %param.9) | copy-start | bytes 9437188
  169.7 116.5 %copy-start.3 = (bf16[128,1024]{1,0:T(8,128)(2,1)S(1)}, bf16[128,1024]{1,0:T(8,128)(2,1)}, u32[]{:S(2)}) copy-start(bf16[128,1024]{1,0:T(8,128)(2,1)} %get-tuple-element.14.back) | copy-start | bytes 786436
  169.7 116.5 %copy-start.5 = (f32[1,5120]{1,0:T(1,128)S(1)}, f32[1,5120]{1,0:T(1,128)}, u32[]{:S(2)}) copy-start(f32[1,5120]{1,0:T(1,128)} %copy-done.4) | copy-start | bytes 61444
  169.7 116.5 %copy-start.6 = (f32[1,5120]{1,0:T(1,128)S(1)}, f32[1,5120]{1,0:T(1,128)}, u32[]{:S(2)}) copy-start(f32[1,5120]{1,0:T(1,128)} %get-tuple-element.19.own.own_hid) | copy-start | bytes 61444
  169.7 116.5 %copy-start.7 = (bf16[128,128]{1,0:T(8,128)(2,1)S(1)}, bf16[128,128]{1,0:T(8,128)(2,1)}, u32[]{:S(2)}) copy-start(bf16[128,128]{1,0:T(8,128)(2,1)} %get-tuple-element.15.back_more) | copy-start | bytes 98308

commit v7 on v6

--- a/solution.py
+++ b/solution.py
@@ -15,6 +15,7 @@
 NARROW = 1024
 VMEM = 56 * 1024 * 1024
 COMBINE_VMEM = 28 * 1024 * 1024
+DOWN_VMEM = 22 * 1024 * 1024
 
 
 def iota(shape, dim):
@@ -275,7 +276,7 @@
         out_specs=pl.BlockSpec((rows, WIDE), lambda i: (0, i)),
         out_shape=jax.ShapeDtypeStruct((rows, width + CHUNK), BF16),
         scratch_shapes=[pltpu.VMEM((rows, CHUNK), BF16), pltpu.VMEM((CHUNK // 128, rows, 128), F32)],
-        compiler_params=pltpu.CompilerParams(vmem_limit_bytes=VMEM),
+        compiler_params=pltpu.CompilerParams(vmem_limit_bytes=DOWN_VMEM),
         cost_estimate=pl.CostEstimate(
             flops=4 * hid.shape[0] * width * half, bytes_accessed=2 * rows * width + 4 * width * half, transcendentals=0
         ),
@@ -290,6 +291,7 @@
         out_specs=anywhere,
         out_shape=jax.ShapeDtypeStruct(value.shape, value.dtype),
         input_output_aliases={0: 0},
+        compiler_params=pltpu.CompilerParams(vmem_limit_bytes=VMEM),
         cost_estimate=pl.CostEstimate(flops=0, bytes_accessed=0, transcendentals=0),
     )(value, *first)
 

time: 299 us -> 301 us (level)
  local copies, waits for them, and re-layouts: 3.95 us -> 8.44 us
    unnamed x20 -> x24, local copies, waits for them, and re-layouts: 3.95 us -> 8.44 us
where the time goes in v7:
time: 301 us; the launch traced here: 297 us
  blocking collectives  237 us (79%)
  Pallas kernels  50.7 us (17%)
  local copies, waits for them, and re-layouts  8.44 us (3%)
    all_to_all x2, blocking collectives, exchange(): lax.all_to_all(value, 'exp', split_axis=0, concat_axis=0, tiled=True)  237 us
    pallas_call x1, Pallas kernels, hidden_units(): pl.pallas_call(functools.partial(hidden_kernel, blocks, slots, extra, chu...  22.1 us
    pallas_call x1, Pallas kernels, down(): pl.pallas_call(functools.partial(down_kernel, blocks, slots, extra, chunk...  11.2 us
    pallas_call x1, Pallas kernels, build(): pl.pallas_call(functools.partial(build_kernel, experts, slots, extra, chu...  10 us
    unnamed x24, local copies, waits for them, and re-layouts  8.44 us
    pallas_call x1, Pallas kernels, combine(): pl.pallas_call(functools.partial(combine_kernel, experts, slots, extra),...  7.36 us
  transfers between devices with their start and end apart: 4, of which 0 were waited for; matrix products, arithmetic and copies ran while one was open for 0% of the time, Pallas kernels for 15%

profile of v7, /device:TPU:50, one launch (start us, length us, event | category | flops | bytes accessed | tf_op | source)
XLA Modules:
  0.0 297.3 jit_solution(3003173410714673833)
XLA Ops:
  0.6 0.1 collective-permute-start
  0.7 0.5 collective-permute-start.1
  1.2 10.0 %shard_map.102 = (bf16[1024,4736]{1,0:T(8,128)(2,1)}, bf16[128,1024]{1,0:T(8,128)(2,1)}, bf16[128,128]{1,0:T(8,128)(2,1)}, bf16[384,4096]{1,0:T(8,128)(2,1)}) custom-call(s32[8,128]{1,0:T(8,128)} %bitcast.33, s32[8,128]{1,0:T(8,128)} %bitcast.34, f32[8,128]{1,0:T(8,128)} %bitcast.35, bf16[128,4096]{1,0:T(8,128)(2,1)} %tok.1, bf16[384,4096]{1,0:T(8,128)(2,1)} %bitcast.16), custom_call_target="tpu_custom_call" | custom-call | flops 2147483648 | bytes 8388608 | tf_op jit(solution)/shard_map/pallas_call | solution.py:108
  11.2 0.0 collective-permute-done.refs_1_.wg1
  11.2 0.0 copy-start.10
  11.3 0.0 collective-permute-done.1.refs_2_.wu1
  11.3 0.0 copy-start.11
  11.3 1.6 copy-done.10
  12.9 1.0 copy-done.11
  13.9 119.6 %all_to_all.10 = bf16[64,16,4736]{2,1,0:T(8,128)(2,1)} all-to-all(bf16[64,16,4736]{2,1,0:T(8,128)(2,1)} %bitcast.25), channel_id=1, replica_groups=mesh['exp'=64,'tp'=2] {'exp'}, dimensions={0} | all-to-all | bytes 19398656 | tf_op jit(solution)/shard_map/all_to_all | solution.py:373
  133.6 0.0 copy-start.1
  133.6 0.0 collective-permute-start.2
  133.6 22.1 %shard_map.104 = (bf16[1152,768]{1,0:T(8,128)(2,1)}, f32[1,5120]{1,0:T(1,128)}) custom-call(bf16[1024,4736]{1,0:T(8,128)(2,1)} %bitcast.27, bf16[1024,4736]{1,0:T(8,128)(2,1)} %bitcast.28, bf16[1024,4736]{1,0:T(8,128)(2,1)} %bitcast.29, bf16[4096,384]{1,0:T(8,128)(2,1)} %bitcast.20, bf16[4096,384]{1,0:T(8,128)(2,1)} %copy-done.10, ...), custom_call_target="tpu_custom_call" | custom-call | flops 14495514624 | bytes 20971520 | tf_op jit(solution)/shard_map/pallas_call | solution.py:212
  155.7 0.2 collective-permute-start.3
  155.9 0.0 collective-permute-done.2.wd1
  156.0 0.0 copy-done.1
  156.0 0.0 copy-start.9
  156.0 1.5 copy-done.9
  157.4 11.2 %shard_map.106.refs_0_ = bf16[1024,4608]{1,0:T(8,128)(2,1)S(1)} custom-call(bf16[1152,768]{1,0:T(8,128)(2,1)S(1)} %copy-done.9, bf16[384,4096]{1,0:T(8,128)(2,1)S(1)} %bitcast.17, bf16[384,4096]{1,0:T(8,128)(2,1)S(1)} %collective-permute-done.2.wd1), custom_call_target="tpu_custom_call" | custom-call | flops 7247757312 | bytes 14680064 | tf_op jit(solution)/shard_map/pallas_call | solution.py:272
  168.6 0.0 copy-start
  168.6 3.6 %copy-done = bf16[1024,4608]{1,0:T(8,128)(2,1)} copy-done((bf16[1024,4608]{1,0:T(8,128)(2,1)}, bf16[1024,4608]{1,0:T(8,128)(2,1)S(1)}, u32[]{:S(2)}) %copy-start) | copy-done | bytes 9437208
  172.3 0.0 collective-permute-done.3.refs_1_.other.other_hid
  172.3 0.0 copy-start.5
  172.3 0.6 copy-done.5
  172.9 0.0 copy-start.2
  172.9 0.0 copy-start.3
  172.9 0.0 copy-start.4
  172.9 0.0 copy-start.6
  172.9 0.0 copy-start.7
  172.9 0.0 copy-start.8
  172.9 117.0 %all_to_all.11 = bf16[64,16,4608]{2,1,0:T(8,128)(2,1)S(1)} all-to-all(bf16[64,16,4608]{2,1,0:T(8,128)(2,1)} %bitcast.15), channel_id=1, replica_groups=mesh['exp'=64,'tp'=2] {'exp'}, dimensions={0} | all-to-all | bytes 18874368 | tf_op jit(solution)/shard_map/all_to_all | solution.py:373
  289.9 0.0 copy-done.2
  289.9 0.0 copy-done.3
  289.9 0.0 copy-done.4
  289.9 0.0 copy-done.6
  289.9 0.0 copy-done.7
  289.9 0.0 copy-done.8
  290.0 7.4 %shard_map.108 = (bf16[128,4096]{1,0:T(8,128)(2,1)}, bf16[4096,384]{1,0:T(8,128)(2,1)}, bf16[4096,384]{1,0:T(8,128)(2,1)}, bf16[384,4096]{1,0:T(8,128)(2,1)}) custom-call(bf16[128,1024]{1,0:T(8,128)(2,1)S(1)} %copy-done.4, bf16[128,128]{1,0:T(8,128)(2,1)S(1)} %copy-done.8, bf16[1024,4608]{1,0:T(8,128)(2,1)S(1)} %bitcast.13, bf16[1024,4608]{1,0:T(8,128)(2,1)S(1)} %bitcast.14, ...), custom_call_target="tpu_custom_call" | custom-call | flops 2147483648 | bytes 28311552 | tf_op jit(solution)/shard_map/pallas_call | solution.py:343
  (3 shorter events, 0.0 us)
Async XLA Ops:
  0.6 10.6 %collective-permute-start = (bf16[4096,384]{1,0:T(8,128)(2,1)}, bf16[4096,384]{1,0:T(8,128)(2,1)S(1)}, u32[]{:S(2)}, u32[]{:S(2)}) collective-permute-start(bf16[4096,384]{1,0:T(8,128)(2,1)} %bitcast.19), channel_id=1, source_target_pairs={{0,1},{1,0},{2,3},{3,2},{4,5},{5,4},{6,7},{7,6},{8,9},{9,8},{10,11... | collective-permute-start | bytes 9437192 | tf_op jit(solution)/shard_map/ppermute | solution.py:368
  0.7 10.5 %collective-permute-start.1 = (bf16[4096,384]{1,0:T(8,128)(2,1)}, bf16[4096,384]{1,0:T(8,128)(2,1)S(1)}, u32[]{:S(2)}, u32[]{:S(2)}) collective-permute-start(bf16[4096,384]{1,0:T(8,128)(2,1)} %bitcast.22), channel_id=1, source_target_pairs={{0,1},{1,0},{2,3},{3,2},{4,5},{5,4},{6,7},{7,6},{8,9},{9,8},{10,11... | collective-permute-start | bytes 9437192 | tf_op jit(solution)/shard_map/ppermute | solution.py:368
  11.2 1.7 copy-start.10
  11.3 2.7 copy-start.11
  133.6 22.4 %copy-start.1 = (bf16[1,384,4096]{2,1,0:T(8,128)(2,1)S(1)}, bf16[1,384,4096]{2,1,0:T(8,128)(2,1)}, u32[]{:S(2)}) copy-start(bf16[1,384,4096]{2,1,0:T(8,128)(2,1)} %param.10) | copy-start | bytes 9437188
  133.6 22.4 %collective-permute-start.2 = (bf16[384,4096]{1,0:T(8,128)(2,1)}, bf16[384,4096]{1,0:T(8,128)(2,1)S(1)}, u32[]{:S(2)}, u32[]{:S(2)}) collective-permute-start(bf16[384,4096]{1,0:T(8,128)(2,1)} %shard_map.105), channel_id=1, source_target_pairs={{0,1},{1,0},{2,3},{3,2},{4,5},{5,4},{6,7},{7,6},{8,9},{9,8},{10,11... | collective-permute-start | bytes 9437192 | tf_op jit(solution)/shard_map/ppermute | solution.py:368
  155.7 16.6 %collective-permute-start.3 = (f32[1,5120]{1,0:T(1,128)}, f32[1,5120]{1,0:T(1,128)S(1)}, u32[]{:S(2)}, u32[]{:S(2)}) collective-permute-start(f32[1,5120]{1,0:T(1,128)} %get-tuple-element.19.own.own_hid), channel_id=1, source_target_pairs={{0,1},{1,0},{2,3},{3,2},{4,5},{5,4},{6,7},{7,6},{8,9},{9,8},{10,11... | collective-permute-start | bytes 61448 | tf_op jit(solution)/shard_map/ppermute | solution.py:368
  156.0 1.5 copy-start.9
  168.6 3.7 %copy-start = (bf16[1024,4608]{1,0:T(8,128)(2,1)}, bf16[1024,4608]{1,0:T(8,128)(2,1)S(1)}, u32[]{:S(2)}) copy-start(bf16[1024,4608]{1,0:T(8,128)(2,1)S(1)} %shard_map.106.refs_0_) | copy-start | bytes 28311556
  172.3 0.6 copy-start.5
  172.9 117.0 %copy-start.2 = (bf16[1,4096,384]{2,1,0:T(8,128)(2,1)S(1)}, bf16[1,4096,384]{2,1,0:T(8,128)(2,1)}, u32[]{:S(2)}) copy-start(bf16[1,4096,384]{2,1,0:T(8,128)(2,1)} %param.8) | copy-start | bytes 9437188
  172.9 117.0 %copy-start.3 = (bf16[1,4096,384]{2,1,0:T(8,128)(2,1)S(1)}, bf16[1,4096,384]{2,1,0:T(8,128)(2,1)}, u32[]{:S(2)}) copy-start(bf16[1,4096,384]{2,1,0:T(8,128)(2,1)} %param.9) | copy-start | bytes 9437188
  172.9 117.0 %copy-start.4 = (bf16[128,1024]{1,0:T(8,128)(2,1)S(1)}, bf16[128,1024]{1,0:T(8,128)(2,1)}, u32[]{:S(2)}) copy-start(bf16[128,1024]{1,0:T(8,128)(2,1)} %get-tuple-element.14.back) | copy-start | bytes 786436
  172.9 117.0 %copy-start.6 = (f32[1,5120]{1,0:T(1,128)S(1)}, f32[1,5120]{1,0:T(1,128)}, u32[]{:S(2)}) copy-start(f32[1,5120]{1,0:T(1,128)} %copy-done.5) | copy-start | bytes 61444
  172.9 117.0 %copy-start.7 = (f32[1,5120]{1,0:T(1,128)S(1)}, f32[1,5120]{1,0:T(1,128)}, u32[]{:S(2)}) copy-start(f32[1,5120]{1,0:T(1,128)} %get-tuple-element.19.own.own_hid) | copy-start | bytes 61444
  172.9 117.0 %copy-start.8 = (bf16[128,128]{1,0:T(8,128)(2,1)S(1)}, bf16[128,128]{1,0:T(8,128)(2,1)}, u32[]{:S(2)}) copy-start(bf16[128,128]{1,0:T(8,128)(2,1)} %get-tuple-element.15.back_more) | copy-start | bytes 98308
